TPU v7x, 32 devices: a whole 2x2x4 slice. The times are simulated.
32 devices in a mesh: wide: 8 (over z, y), narrow: 4 (over x, core).
Axes of the slice: x: 2, y: 2, z: 4, core: 2. Of those that a mesh axis runs over, the one named last changes fastest.
Arguments:
- tokens: bfloat16 [26624, 768], P(('wide', 'narrow')), may hold values from -6 to 6
- kinds: int32 [26624], P(('wide', 'narrow')), may hold values from 0 to 1
- lengths: int32 [128], P(('wide', 'narrow')), may hold values from 52 to 208, as said below
- query_weight: bfloat16 [768, 768], replicated, may hold values from -0.21875 to 0.21875
- key_weight: bfloat16 [768, 768], replicated, may hold values from -0.21875 to 0.21875
- value_weight: bfloat16 [768, 768], replicated, may hold values from -0.21875 to 0.21875
- output_weight: bfloat16 [768, 768], replicated, may hold values from -0.875 to 0.875
- inner_weight: bfloat16 [768, 768], replicated, may hold values from -0.21875 to 0.21875
- outer_weight: bfloat16 [768, 768], replicated, may hold values from -0.21875 to 0.21875
- query_bias: bfloat16 [768], replicated, may hold values from -1 to 1
- value_bias: bfloat16 [768], replicated, may hold values from -1 to 1
- output_bias: bfloat16 [768], replicated, may hold values from -1 to 1
- inner_bias: bfloat16 [768], replicated, may hold values from -1 to 1
- outer_bias: bfloat16 [768], replicated, may hold values from -1 to 1
- first_gain: bfloat16 [768], replicated, may hold values from 0.5 to 1.5
- first_shift: bfloat16 [768], replicated, may hold values from -1 to 1
- second_gain: bfloat16 [768], replicated, may hold values from 0.5 to 1.5
- second_shift: bfloat16 [768], replicated, may hold values from -1 to 1
- type_table: bfloat16 [2, 768], replicated, may hold values from -3 to 3
- cotangent: bfloat16 [26624, 768], P(('wide', 'narrow')), may hold values from -6 to 6
Outputs:
- layer_out: bfloat16 [26624, 768], P(('wide', 'narrow'))
- tokens_grad: bfloat16 [26624, 768], P(('wide', 'narrow'))
- query_grad: float32 [768, 768], replicated
- key_grad: float32 [768, 768], replicated
- value_grad: float32 [768, 768], replicated
- output_grad: float32 [768, 768], replicated
- inner_grad: float32 [768, 768], replicated
- outer_grad: float32 [768, 768], replicated
- query_bias_grad: float32 [768], replicated
- value_bias_grad: float32 [768], replicated
- output_bias_grad: float32 [768], replicated
- inner_bias_grad: float32 [768], replicated
- outer_bias_grad: float32 [768], replicated
- first_gain_grad: float32 [768], replicated
- first_shift_grad: float32 [768], replicated
- second_gain_grad: float32 [768], replicated
- second_shift_grad: float32 [768], replicated
- table_grad: float32 [2, 768], replicated
Inputs may be any that keep to these rules, and one draw needn't show every extreme that they name: `lengths`: tokens of each molecule; the remaining of its 208 slots are padding. `kinds`: 0 marks a node token, 1 an edge token.
All inputs are finite; a program needn't handle non-finite values.
Results may differ from a plain program's by a relative error of at most 0.012.
Values sent between devices are 32-bit elements; how exact they have to be, the bound alone decides.
No kernel may reach another device: no remote copies, remote signals or barrier semaphores. Data moves between devices by JAX's collectives and lax.ppermute only.
A program may use at most 192 MiB of HBM per device.

v0:
```python
import functools
import math

import jax
import jax.numpy as jnp
import numpy as np
from jax import lax
from jax.experimental import pallas as pl
from jax.experimental.pallas import tpu as pltpu
from jax.sharding import PartitionSpec as P

D = 768
H = 32
DH = 24
SLOT = 208
GROUP = 16
HALF = GROUP * DH
WIDE = 256
SCALE = 1.0 / math.sqrt(DH)
LOG_SCALE = math.log2(math.e) / math.sqrt(DH)
LN_2 = math.log(2.0)
AXES = ("wide", "narrow")
NN = (((1,), (0,)), ((), ()))
NT = (((1,), (1,)), ((), ()))
TN = (((0,), (0,)), ((), ()))
F32 = jnp.float32
BF16 = jnp.bfloat16
VMEM = 60 * 2**20
HBM = pl.BlockSpec(memory_space=pltpu.HBM)


SCHEDULE = "FwDAx0OA1yOAzBOCAIOBACOBACBOACOBCBACOBOAoaCBBbCqCr"


def dot(left, right, dims=NN):
    return lax.dot_general(left, right, dims, preferred_element_type=F32)


def norm_parts(values):
    average = jnp.mean(values, -1, keepdims=True)
    centered = values - average
    inv_std = lax.rsqrt(jnp.mean(centered * centered, -1, keepdims=True) + 1e-05)
    return centered * inv_std, inv_std


def norm_back(grad_hat, normed, inv_std):
    return (
        grad_hat
        - jnp.mean(grad_hat, -1, keepdims=True)
        - normed * jnp.mean(grad_hat * normed, -1, keepdims=True)
    ) * inv_std


def row_of(ref):
    return ref[...].astype(F32).reshape(1, D)


def kinds_column(kinds_ref, edge_ref):
    @pl.when(pl.program_id(0) == 0)
    def turn():
        kinds = kinds_ref[...].astype(F32).reshape(1, -1)
        edge_ref[...] = jnp.broadcast_to(kinds, (8, kinds.shape[1])).T[:, :1]


def embed(tokens, edge, table_ref):
    table = table_ref[...].astype(F32)
    return tokens.astype(F32) + jnp.where(edge == 1, table[1:2], table[0:1])


def turn(values):
    return jnp.concatenate([values, jnp.zeros((WIDE - SLOT, values.shape[1]), F32)]).T


def with_rows(values, rows):
    index = lax.broadcasted_iota(jnp.int32, (8, WIDE), 0)
    extra = jnp.zeros((8, WIDE), F32)
    for i, row in enumerate(rows):
        extra = jnp.where(index == i, row, extra)
    if values.ndim == 3:
        extra = jnp.broadcast_to(extra, (values.shape[0], 8, WIDE))
    return jnp.concatenate([values, extra], -2).astype(BF16)


def split_row(row):
    high = row.astype(BF16).astype(F32)
    mid = (row - high).astype(BF16).astype(F32)
    return [high, mid, row - high - mid]


def attend_kernel(
    factor, lengths_ref, place_ref, tokens_ref, kinds_ref, table_ref, gain_ref, shift_ref, query_bias_ref,
    value_bias_ref, query_weight_ref, key_weight_ref, value_weight_ref, output_bias_ref, inner_bias_ref,
    second_gain_ref, second_shift_ref, *refs,
):
    later_hbm, refs = refs[:5], refs[5:]
    first_ref, query_ref, keys_ref, values_ref, mixed_ref, stat_ref, *outputs = refs[:11]
    edge_ref, scores_ref, out_ref, mixed_all_ref, second_ref, *later, sems = refs[11:]
    mol = pl.program_id(0)
    copies = [pltpu.make_async_copy(*pair, sems.at[k]) for k, pair in enumerate(zip(later_hbm, later))]

    @pl.when(mol == 0)
    def fetch():
        for copy in copies:
            copy.start()

    kinds_column(kinds_ref, edge_ref)

    @pl.when(mol < pl.num_programs(0) - 1)
    def attend():
        attend_molecule(
            mol, lengths_ref, tokens_ref, edge_ref, table_ref, gain_ref, shift_ref, query_bias_ref, value_bias_ref,
            query_weight_ref, key_weight_ref, value_weight_ref, first_ref, query_ref, keys_ref, values_ref, mixed_ref,
            stat_ref, scores_ref, out_ref,
        )
        mixed_all_ref[mol] = mixed_ref[0]

    @pl.when(mol == pl.num_programs(0) - 1)
    def forward():
        for copy in copies:
            copy.wait()
        feed_forward(
            factor, lengths_ref, place_ref, edge_ref, table_ref, mixed_all_ref, *later, output_bias_ref,
            inner_bias_ref, second_gain_ref, second_shift_ref, *outputs, second_ref,
        )


def attend_molecule(
    mol, lengths_ref, tokens_ref, edge_ref, table_ref, gain_ref, shift_ref, query_bias_ref, value_bias_ref,
    query_weight_ref, key_weight_ref, value_weight_ref, first_ref, query_ref, keys_ref, values_ref, mixed_ref,
    stat_ref, scores_ref, out_ref,
):
    edge = edge_ref[pl.ds(pl.multiple_of(mol * SLOT, 8), SLOT), :]
    normed, unused = norm_parts(embed(tokens_ref[...], edge, table_ref))
    first32 = normed * row_of(gain_ref) + row_of(shift_ref)
    first = first32.astype(BF16)
    first_ref[0] = turn(first32).astype(BF16)
    slot = lax.broadcasted_iota(jnp.int32, (1, WIDE), 1)
    bias = jnp.where(slot < lengths_ref[mol], 0.0, -1e30)
    ones = jnp.ones((1, WIDE), F32)
    query = (dot(first, query_weight_ref[...]) + row_of(query_bias_ref)) * LOG_SCALE
    keys = dot(first, key_weight_ref[...])
    values = dot(first, value_weight_ref[...]) + row_of(value_bias_ref)
    query_ref[0] = with_rows(turn(query).reshape(H, DH, WIDE), [ones])
    keys_ref[0] = with_rows(turn(keys).reshape(H, DH, WIDE), [bias, ones, ones, ones])
    values_ref[0] = with_rows(turn(values).reshape(H, DH, WIDE), [ones, ones, ones])
    lag = 7

    def score(h):
        scores_ref[h % (lag + 1)] = dot(keys_ref[0, h, :, :SLOT], query_ref[0, h], TN)

    def mix(h):
        scores = scores_ref[h % (lag + 1)]
        top = jnp.max(scores, axis=0, keepdims=True)
        powered = jnp.exp2(scores - top).astype(BF16)
        out = dot(values_ref[0, h, :, :SLOT], powered)
        total = out[DH : DH + 1]
        out_ref[h * DH : (h + 1) * DH, :] = out[:DH] * (1.0 / total)
        stat_ref[0, h // GROUP, h % GROUP : h % GROUP + 1] = top + jnp.log2(total)

    for h in range(H + lag):
        if h < H:
            score(h)
        if h >= lag:
            mix(h - lag)
    mixed_ref[0] = out_ref[...].astype(BF16)


def gelu_parts(inner):
    root = math.sqrt(2.0 / math.pi)
    bend = root * 0.044715 * inner * inner + root
    half = 0.5 * jnp.tanh(inner * bend) + 0.5
    act = inner * half
    return act, half + act * (1.0 - half) * (6.0 * bend - 4.0 * root)


def valid_rows(lengths_ref, first, mols):
    slot = lax.broadcasted_iota(jnp.int32, (SLOT, 1), 0)
    return jnp.concatenate([(slot < lengths_ref[first + i]).astype(F32) for i in range(mols)])


def feed_forward(
    factor, lengths_ref, place_ref, edge_ref, table_ref, mixed_ref, tokens_ref, cotangent_ref, output_weight_ref,
    inner_weight_ref, outer_weight_ref, output_bias_ref, inner_bias_ref, gain_ref, shift_ref,
    middle_ref, act_ref, grad_inner_ref, kept_ref, sent_ref, second_ref,
):
    mols = mixed_ref.shape[0]
    edge = edge_ref[...]
    valid = valid_rows(lengths_ref, 0, mols)
    mixed = jnp.concatenate([dot(mixed_ref[i], output_weight_ref[...], TN)[:SLOT] for i in range(mols)])
    middle = embed(tokens_ref[...], edge, table_ref) + mixed + row_of(output_bias_ref)
    middle_ref[...] = middle
    normed, unused = norm_parts(middle)
    second = (normed * row_of(gain_ref) + row_of(shift_ref)).astype(BF16)
    inner = dot(second, inner_weight_ref[...]) + row_of(inner_bias_ref)
    act32, slope = gelu_parts(inner)
    act = act32.astype(BF16)
    act_ref[...] = act
    grad_low = (cotangent_ref[...].astype(F32) * valid).astype(BF16)
    grad_inner = (dot(grad_low, outer_weight_ref[...], NT) * slope).astype(BF16)
    grad_inner_ref[...] = grad_inner

    second_ref[...] = second
    for target, begin in core_halves(place_ref[0], kept_ref, sent_ref):
        target[:, :D] = dot(act_ref[:, pl.ds(begin, D // 2)], grad_low * BF16(factor), TN)
        target[:, D:] = dot(second_ref[:, pl.ds(begin, D // 2)], grad_inner * BF16(factor), TN)


def core_halves(core, kept_ref, sent_ref):
    rows = kept_ref.shape[0]
    return [(ref, pl.multiple_of(which * rows, 128)) for ref, which in ((kept_ref, core), (sent_ref, 1 - core))]


def backward_kernel(
    factor, lengths_ref, place_ref, middle_ref, act_ref, grad_inner_ref, mixed_ref, cotangent_ref, outer_bias_ref,
    gain_ref, output_weight_ref, inner_weight_ref, outer_weight_ref,
    layer_ref, grad_middle_ref, grad_mixed_ref, kept_ref, sent_ref, vectors_ref,
):
    mols = mixed_ref.shape[0]
    valid = valid_rows(lengths_ref, 0, mols)
    middle = middle_ref[...]
    normed, inv_std = norm_parts(middle)
    grad_out = cotangent_ref[...].astype(F32) * valid
    grad_inner = grad_inner_ref[...]
    grad_second = dot(grad_inner, inner_weight_ref[...], NT)
    grad_middle = grad_out + norm_back(grad_second * row_of(gain_ref), normed, inv_std)
    grad_middle_ref[...] = grad_middle
    pad = jnp.zeros((WIDE - SLOT, D), F32)
    grads = [jnp.concatenate([grad_middle[i * SLOT : (i + 1) * SLOT], pad]).astype(BF16) for i in range(mols)]
    for i, grad in enumerate(grads):
        grad_mixed_ref[i] = dot(output_weight_ref[...], grad, NT).astype(BF16)
    for target, begin in core_halves(place_ref[0], kept_ref, sent_ref):
        products = [dot(mixed_ref[i, pl.ds(begin, D // 2), :], grad * BF16(factor)) for i, grad in enumerate(grads)]
        target[...] = functools.reduce(jnp.add, products)
    layer = middle + dot(act_ref[...], outer_weight_ref[...]) + row_of(outer_bias_ref)
    layer_ref[...] = (layer * valid).astype(BF16)
    sums = [
        grad_out,
        grad_inner.astype(F32),
        grad_second * normed,
        grad_second,
        grad_middle.astype(BF16).astype(F32),
    ]
    vectors_ref[...] = jnp.zeros_like(vectors_ref)
    for i, values in enumerate(sums):
        vectors_ref[i : i + 1] = jnp.sum(values, 0, keepdims=True) * factor


def back_kernel(
    factor, lengths_ref, place_ref, first_ref, query_ref, keys_ref, values_ref, mixed_ref, grad_ref, stat_ref,
    vectors_ref, turned_grads_ref, kept_ref, sent_ref,
    mixed32_ref, grad32_ref, scores_ref, probs_ref, grads_ref,
):
    step = pl.program_id(0)

    @pl.when(step == 0)
    def start_sums():
        for ref in (grads_ref, kept_ref, sent_ref, vectors_ref):
            ref[...] = jnp.zeros_like(ref)

    mixed32_ref[...] = mixed_ref[0].astype(F32)
    grad32_ref[...] = grad_ref[0].astype(F32)
    lag = 2

    def score(h):
        rows = slice(h * DH, (h + 1) * DH)
        stat = split_row(-stat_ref[0, 0, h : h + 1])
        query = with_rows(query_ref[0, h].astype(F32)[:DH], [1.0] + stat)
        scores_ref[h % (lag + 1)] = dot(keys_ref[0, h, :, :SLOT], query, TN)
        grad = grad32_ref[rows]
        shared = split_row(-jnp.sum(grad * mixed32_ref[rows], axis=0, keepdims=True))
        probs_ref[h % (lag + 1)] = dot(values_ref[0, h, :, :SLOT], with_rows(grad, shared), TN)

    def back(h):
        rows = slice(h * DH, (h + 1) * DH)
        probs = jnp.exp2(scores_ref[h % (lag + 1)])
        grad_scores = (probs * probs_ref[h % (lag + 1)]).astype(BF16)
        grad = with_rows(grad32_ref[rows], [])
        grads_ref[0, rows] = dot(keys_ref[0, h, :, :SLOT], grad_scores)[:DH] * SCALE
        grads_ref[1, rows, :SLOT] = dot(query_ref[0, h], grad_scores, NT)[:DH] * LN_2
        grads_ref[2, rows, :SLOT] = dot(grad, probs.astype(BF16), NT)[:DH]

    for h in range(GROUP + lag):
        if h < GROUP:
            score(h)
        if h >= lag:
            back(h - lag)
    grads = grads_ref[...].astype(BF16)
    turned_grads_ref[0] = grads
    grads = (grads * BF16(factor)).reshape(3 * HALF, WIDE)
    for target, begin in core_halves(place_ref[0], kept_ref, sent_ref):
        target[...] += dot(first_ref[0, pl.ds(begin, D // 2), :], grads, NT)
    vectors_ref[...] += dot(jnp.ones((8, WIDE), BF16), grads, NT)


def input_kernel(
    factor, lengths_ref, place_ref, tokens_ref, kinds_ref, table_ref, gain_ref, low_ref, high_ref, query_weight_ref,
    key_weight_ref, value_weight_ref, grad_middle_ref, dense_ref, low_bias_ref, high_bias_ref,
    tokens_grad_ref, vectors_ref,
    edge_ref,
):
    mol = pl.program_id(0)

    @pl.when(mol == 0)
    def start_sums():
        vectors_ref[...] = jnp.zeros_like(vectors_ref)

    kinds_column(kinds_ref, edge_ref)
    edge = edge_ref[pl.ds(pl.multiple_of(mol * SLOT, 8), SLOT), :]
    total = jnp.zeros((D, WIDE), F32)
    for i, weight_ref in enumerate((query_weight_ref, key_weight_ref, value_weight_ref)):
        total = total + dot(weight_ref[...], jnp.concatenate([low_ref[0, i], high_ref[0, i]]))
    grad_first = total.T[:SLOT]
    normed, inv_std = norm_parts(embed(tokens_ref[...], edge, table_ref))
    grad_start = grad_middle_ref[...] + norm_back(grad_first * row_of(gain_ref), normed, inv_std)
    tokens_grad_ref[...] = grad_start.astype(BF16)
    sums = [
        grad_first * normed,
        grad_first,
        jnp.where(edge == 1, 0.0, grad_start),
        jnp.where(edge == 1, grad_start, 0.0),
    ]
    for i, values in enumerate(sums):
        vectors_ref[i : i + 1] += jnp.sum(values, 0, keepdims=True)

    @pl.when(mol == pl.num_programs(0) - 1)
    def finish():
        vectors_ref[...] = vectors_ref[...] * factor
        for i, begin in ((0, 0), (1, 2 * HALF)):
            vectors_ref[4 + i : 5 + i, :HALF] = low_bias_ref[:1, begin : begin + HALF]
            vectors_ref[4 + i : 5 + i, HALF:] = high_bias_ref[:1, begin : begin + HALF]
        vectors_ref[8:16] = dense_ref[...]


def whole(*shape):
    return pl.BlockSpec(shape, lambda i, *_: (0,) * len(shape))


def rows_of(width):
    return pl.BlockSpec((SLOT, width), lambda i, *_: (i, 0))


def mols_of(*shape):
    return pl.BlockSpec((1,) + shape, lambda i, *_: (i,) + (0,) * len(shape))


def shape_of(*shape, dtype=F32):
    return jax.ShapeDtypeStruct(shape, dtype)


def call(kernel, count, in_specs, out_specs, out_shape, scratch, args, flops, name, vmem=VMEM):
    return pl.pallas_call(
        kernel,
        grid_spec=pltpu.PrefetchScalarGridSpec(
            num_scalar_prefetch=2,
            grid=(count,),
            in_specs=in_specs,
            out_specs=out_specs,
            scratch_shapes=scratch,
        ),
        out_shape=out_shape,
        compiler_params=pltpu.CompilerParams(
            dimension_semantics=("arbitrary",), vmem_limit_bytes=vmem
        ),
        cost_estimate=pl.CostEstimate(flops=20 * flops, bytes_accessed=2**20, transcendentals=0),
        name=name,
    )(*args)


def bits_of(mesh_shape):
    narrow = mesh_shape["narrow"].bit_length() - 1
    wide = mesh_shape["wide"].bit_length() - 1
    y = (wide - 1) // 2
    return {
        "c": [0],
        "x": list(range(1, narrow)),
        "y": list(range(narrow, narrow + y)),
        "z": list(range(narrow + y, narrow + wide)),
    }


def swap(values, bit, devices):
    even, odd = bit if isinstance(bit, tuple) else (bit, bit)
    return lax.ppermute(values, AXES, [(i, i ^ (1 << (odd if i & 1 else even))) for i in range(devices)])


def pick(values, *index):
    for i in index:
        values = lax.dynamic_index_in_dim(values, i, 0, keepdims=False)
    return values


def place_kernel(parts, count_in, place_ref, *refs):
    sources = refs[: len(parts)]
    outs, sems = refs[len(parts) + count_in : -1], refs[-1]
    stores = []
    for n, (other, low, targets, column) in enumerate(parts):
        core, first, second = place_ref[0], place_ref[1], place_ref[2]
        if other:
            core, first, second = 1 - core, second, first
        rows = D // 16
        width = sources[n].shape[1] // len(targets)
        for k in range(4):
            row = (
                core,
                lax.bitwise_xor(low, first),
                lax.bitwise_xor(k // 2, second),
                lax.bitwise_xor(k % 2, place_ref[3]),
            )
            for m, target in enumerate(targets):
                stores.append(
                    pltpu.make_async_copy(
                        sources[n].at[k * rows : (k + 1) * rows, m * width : (m + 1) * width],
                        outs[target].at[*row, :, column : column + width],
                        sems.at[n, k, m],
                    )
                )
                stores[-1].start()
    for store in stores:
        store.wait()


def put_in_place(place, pieces, parts, count_out, before=()):
    rows = D // 16
    pieces = [piece.reshape(-1, piece.shape[-1]) for piece in pieces]
    return pl.pallas_call(
        functools.partial(place_kernel, parts, len(before)),
        grid_spec=pltpu.PrefetchScalarGridSpec(
            num_scalar_prefetch=1,
            grid=(1,),
            in_specs=[whole(*piece.shape) for piece in pieces] + [HBM] * len(before),
            out_specs=[HBM] * count_out,
            scratch_shapes=[pltpu.SemaphoreType.DMA((len(pieces), 4, 3))],
        ),
        out_shape=[shape_of(2, 2, 2, 2, rows, D)] * count_out,
        input_output_aliases={1 + len(pieces) + i: i for i in range(len(before))},
        compiler_params=pltpu.CompilerParams(vmem_limit_bytes=20 * 2**20),
        cost_estimate=pl.CostEstimate(flops=10**10, bytes_accessed=2**20, transcendentals=0),
        name="place",
    )(place, *pieces, *before)


def spread_sum(kept, sent, rider, own, bits, me, devices):
    rows, width = kept.shape[0] // 8, kept.shape[1]
    core, x, y, z = (bits[k][0] for k in "cxyz")
    (got,) = yield [(sent, core)]
    terms = [v.reshape(2, 2, 2, rows, width) for v in (kept, got)]
    scatter = (((x, y), me[1]), ((y, x), me[2]), (z, me[3]))
    for bit, mine in scatter:
        (got,) = yield [(functools.reduce(jnp.add, [pick(t, 1 - mine) for t in terms]), bit)]
        terms = [pick(t, mine) for t in terms] + [got]
    total = functools.reduce(jnp.add, terms)
    small = rider()

    def with_small(values):
        return values if small is None else jnp.concatenate([values.reshape(-1, width), small])

    def apart(values, shape):
        if small is None:
            return values, None
        count = math.prod(shape[:-1])
        return values[:count].reshape(shape), small + values[count:]

    for bit in bits["x"][1:] + bits["y"][1:] + bits["z"][1:]:
        (got,) = yield [(with_small(total), bit)]
        got, small = apart(got, total.shape)
        total = total + got
    (got,) = yield [(with_small(total), z)]
    got, small = apart(got, total.shape)
    total = jnp.stack([total, got])
    (got,) = yield [(with_small(total), (y, x))]
    got, small = apart(got, total.shape)
    total = jnp.stack([total, got])
    got, other = yield [(with_small(total), (x, y)), (total, core)]
    got, small = apart(got, total.shape)
    own.extend((total, got))
    (last,) = yield [(with_small(got), core)]
    if small is not None:
        small = small + last[-small.shape[0] :]
    yield (other, last), small


class Order:
    def __init__(self):
        self.before = ()

    def after(self, *values):
        if self.before:
            values, unused = lax.optimization_barrier((values, self.before))
        return values

    def add(self, *values):
        self.before = tuple(values)


class Transfer:
    def __init__(self, name, steps, own, devices, order):
        self.name = name
        self.own = own
        self.level = 0
        self.steps = steps
        self.devices = devices
        self.order = order
        self.result = None
        self.send(next(self.steps))

    def send(self, sent):
        self.order.add(*self.order.before, *[values for values, unused in sent])
        with jax.named_scope(f"{self.name}_{self.level}"):
            self.got = [swap(values, bit, self.devices) for values, bit in sent]
        self.level += 1

    def go(self):
        if self.result is not None:
            return
        sent = self.steps.send(self.order.after(*self.got))
        if isinstance(sent, list):
            self.order.before = ()
            self.send(sent)
        else:
            self.result = sent


def per_device(
    mesh_shape, tokens, kinds, lengths, query_weight, key_weight, value_weight, output_weight, inner_weight,
    outer_weight, query_bias, value_bias, output_bias, inner_bias, outer_bias, first_gain, first_shift,
    second_gain, second_shift, type_table, cotangent,
):
    count = lengths.shape[0]
    rows = tokens.shape[0]
    devices = mesh_shape["wide"] * mesh_shape["narrow"]
    factor = 1.0 / devices
    bits = bits_of(mesh_shape)
    index = lax.axis_index("wide") * mesh_shape["narrow"] + lax.axis_index("narrow")
    at = [(index >> bits[k][0]) & 1 for k in "cxyz"]
    me = [at[0], jnp.where(at[0] == 0, at[1], at[2]), jnp.where(at[0] == 0, at[2], at[1]), at[3]]
    place = jnp.stack(me).astype(jnp.int32)
    unit = 2 * rows * D * D
    attention = 2 * rows * SLOT * D
    vec = pl.BlockSpec((D,), lambda i, *_: (0,))
    weight = whole(D, D)
    edges = pl.BlockSpec((rows,), lambda i, *_: (0,))
    column = pltpu.VMEM((rows, 1), F32)
    scalars = (lengths, place)
    once = pl.Buffered(1)
    single = lambda *shape: pl.BlockSpec(shape, lambda i, *_: (0,) * len(shape), pipeline_mode=once)
    now = lambda *shape: pl.BlockSpec((1,) + shape, lambda i, *_: (jnp.minimum(i, count - 1),) + (0,) * len(shape))
    low = pltpu.VMEM((rows, D), BF16)
    room = pltpu.VMEM((D, D), BF16)
    first, query, keys, values, mixed, stat, middle, act, grad_inner, *dense_parts = call(
        functools.partial(attend_kernel, factor), count + 1,
        [pl.BlockSpec((SLOT, D), lambda i, *_: (jnp.minimum(i, count - 1), 0)), edges, whole(2, D), vec, vec, vec, vec,
         single(D, D), single(D, D), single(D, D), vec, vec, vec, vec] + [HBM] * 5,
        [now(D, WIDE)] + [now(H, 32, WIDE)] * 3 + [now(D, WIDE), now(2, GROUP, WIDE)] + [single(rows, D)] * 3
        + [single(D // 2, 2 * D)] * 2,
        [shape_of(count, D, WIDE, dtype=BF16)] + [shape_of(count, H, 32, WIDE, dtype=BF16)] * 3
        + [shape_of(count, D, WIDE, dtype=BF16), shape_of(count, 2, GROUP, WIDE), shape_of(rows, D),
           shape_of(rows, D, dtype=BF16), shape_of(rows, D, dtype=BF16)] + [shape_of(D // 2, 2 * D)] * 2,
        [column, pltpu.VMEM((8, SLOT, WIDE), F32), pltpu.VMEM((D, WIDE), F32), pltpu.VMEM((count, D, WIDE), BF16), low,
         low, low, room, room, room, pltpu.SemaphoreType.DMA((5,))],
        (*scalars, tokens, kinds, type_table, first_gain, first_shift, query_bias, value_bias, query_weight,
         key_weight, value_weight, output_bias, inner_bias, second_gain, second_shift, tokens, cotangent,
         output_weight, inner_weight, outer_weight),
        flops=8 * unit + 20 * attention, name="attend",
    )
    mols = count
    tall = lambda width: pl.BlockSpec((mols * SLOT, width), lambda i, *_: (i, 0))
    several = pl.BlockSpec((mols, D, WIDE), lambda i, *_: (i, 0, 0))
    halves = lambda width: [whole(D // 2, width)] * 2
    half_shapes = lambda width: [shape_of(D // 2, width)] * 2
    wide = 3 * HALF
    order = Order()
    transfers, made, placed = {}, {}, {}

    def begin(name):
        kept, sent = made[name]
        (sent,) = order.after(sent)
        order.before = ()
        rider = (lambda: made["input"][1]) if name == "O" else (lambda: None)
        own = []
        steps = spread_sum(kept, sent, rider, own, bits, me, devices)
        transfers[name] = Transfer(f"sum_{name}", steps, own, devices, order)

    def spread(name, *parts):
        made[name] = parts

    def dense_forward():
        order.add(act)
        spread("A", *dense_parts)

    def dense_backward():
        (act_in,) = order.after(act)
        layer_out, grad_middle, grad_mixed, *parts, dense_vectors = call(
            functools.partial(backward_kernel, factor), count // mols,
            [tall(D), tall(D), tall(D), several, tall(D), vec, vec, weight, weight, weight],
            [tall(D), tall(D), several] + halves(D) + [whole(8, D)],
            [shape_of(rows, D, dtype=BF16), shape_of(rows, D), shape_of(count, D, WIDE, dtype=BF16)] + half_shapes(D)
            + [shape_of(8, D)],
            [],
            (*scalars, middle, act_in, grad_inner, mixed, cotangent, outer_bias, second_gain, output_weight,
             inner_weight, outer_weight),
            flops=4 * unit, name="dense_backward",
        )
        made["backward"] = layer_out, grad_middle, grad_mixed, dense_vectors
        order.add(dense_vectors)
        spread("O", *parts)

    def back(part):
        heads = pl.BlockSpec((1, GROUP, 32, WIDE), lambda i, *_: (i, part, 0, 0))
        half = pl.BlockSpec((1, HALF, WIDE), lambda i, *_: (i, part, 0))
        (grad_in,) = order.after(made["backward"][2])
        bias_grad, turned_grads, *parts = call(
            functools.partial(back_kernel, factor), count,
            [mols_of(D, WIDE), heads, heads, heads, half, half,
             pl.BlockSpec((1, 1, GROUP, WIDE), lambda i, *_: (i, part, 0, 0))],
            [whole(8, wide), mols_of(3, HALF, WIDE)] + halves(wide),
            [shape_of(8, wide), shape_of(count, 3, HALF, WIDE, dtype=BF16)] + half_shapes(wide),
            [pltpu.VMEM((HALF, WIDE), F32)] * 2 + [pltpu.VMEM((3, SLOT, WIDE), F32)] * 2
            + [pltpu.VMEM((3, HALF, WIDE), F32)],
            (*scalars, first, query, keys, values, mixed, grad_in, stat),
            flops=unit + 20 * attention, name=f"back_{part}",
        )
        made[part] = turned_grads, bias_grad
        order.add(bias_grad)
        spread("BC"[part], *parts)

    def to_input():
        layer_out, grad_middle, grad_mixed, dense_vectors = made["backward"]
        (grad_middle,) = order.after(grad_middle)
        made["input"] = call(
            functools.partial(input_kernel, factor), count,
            [rows_of(D), edges, whole(2, D), vec, mols_of(3, HALF, WIDE), mols_of(3, HALF, WIDE), weight, weight,
             weight, rows_of(D), whole(8, D), whole(8, wide), whole(8, wide)],
            [rows_of(D), whole(16, D)],
            [shape_of(rows, D, dtype=BF16), shape_of(16, D)],
            [column],
            (*scalars, tokens, kinds, type_table, first_gain, made[0][0], made[1][0], query_weight, key_weight,
             value_weight, grad_middle, dense_vectors, made[0][1], made[1][1]),
            flops=3 * unit, name="input", vmem=40 * 2**20,
        )
        order.add(made["input"][1])

    def own_parts(name, targets, column=0):
        while not transfers[name].own:
            transfers[name].go()
        return [(piece, (0, low, targets, column)) for low, piece in enumerate(transfers[name].own)]

    def other_parts(name, targets, column=0):
        while transfers[name].result is None:
            transfers[name].go()
        return [(piece, (1, low, targets, column)) for low, piece in enumerate(transfers[name].result[0])]

    def into_place(step):
        before, three = (), (0, 1, 2)
        if step == "a":
            found = other_parts("A", (0, 1)) + own_parts("A", (0, 1))
        elif step == "o":
            found = other_parts("O", (0,)) + own_parts("O", (0,))
        elif step == "b":
            found = other_parts("B", three) + own_parts("B", three)
        elif step == "q":
            found, before = own_parts("C", three, HALF), placed["b"]
        else:
            found, before = other_parts("C", three, HALF), placed["q"]
        pieces, parts = zip(*found)
        placed[step] = put_in_place(
            place, order.after(*pieces), parts, {"a": 2, "o": 1}.get(step, 3), before
        )
        order.add(placed[step][0])

    def finish_vectors():
        if "vectors" not in made:
            small = transfers["O"].result[1]
            made["vectors"] = [small[i] for i in (4, 5, 12, 9, 8, 0, 1, 10, 11)] + [small[2:4]]
            order.add(*order.before, *made["vectors"])

    kernels = {"F": dense_forward, "D": dense_backward, "0": lambda: back(0), "1": lambda: back(1), "I": to_input}
    for step in SCHEDULE:
        if step in kernels:
            kernels[step]()
        elif step in "wxyz":
            begin("AOBC"["wxyz".index(step)])
        elif step in transfers:
            transfers[step].go()
            if step == "O" and transfers[step].result is not None:
                finish_vectors()
        else:
            into_place(step)
    outer_grad, inner_grad = placed["a"]
    (output_grad,) = placed["o"]
    query_grad, key_grad, value_grad = placed["r"]
    layer_out = made["backward"][0]
    tokens_grad = made["input"][0]
    finish_vectors()
    return tuple(
        [layer_out, tokens_grad]
        + [grad.reshape(D, D) for grad in (query_grad, key_grad, value_grad, output_grad, inner_grad, outer_grad)]
        + made["vectors"]
    )


def solution(mesh):
    split = P(AXES, None)
    return jax.shard_map(
        functools.partial(per_device, dict(mesh.shape)),
        mesh=mesh,
        in_specs=(split, P(AXES), P(AXES)) + (P(),) * 16 + (split,),
        out_specs=(split, split) + (P(),) * 16,
        check_vma=False,
    )
```

profile of v0, /device:TPU:0, one launch (start us, length us, event | category | flops | bytes accessed | tf_op | source)
XLA Modules:
  0.0 203.7 jit_solution(14676421893672529531)
XLA Ops:
  1.3 25.9 %attend.1 = (bf16[4,768,256]{2,1,0:T(8,128)(2,1)}, bf16[4,32,32,256]{3,2,1,0:T(8,128)(2,1)}, bf16[4,32,32,256]{3,2,1,0:T(8,128)(2,1)}, bf16[4,32,32,256]{3,2,1,0...) custom-call(s32[4]{0:T(128)} %lengths_ref.9, ...), custom_call_target="tpu_custom_call" | custom-call | flops 263360348160 | bytes 1048576 | tf_op jit(solution)/shard_map/attend/pallas_call | solution.py:351
  27.7 12.3 %dense_backward.1 = (bf16[832,768]{1,0:T(8,128)(2,1)}, f32[832,768]{1,0:T(8,128)}, bf16[4,768,256]{2,1,0:T(8,128)(2,1)}, f32[384,768]{1,0:T(8,128)}, f32[384,768]{1,0:T(8,128)}, /*index=5*/f32[8,768]{1,0:T(8,128)}) custom-call(s32[4]{0:T(128)} %lengths_ref.9, s32[4]{0:T(128)} %pad_add_fusion.place_ref, f32[832,768]{1,0:T(8,128)} %get-tuple-element.120.middle_ref, ...), custom_call_target="tpu_custom_call" | custom-call | flops 78517370880 | bytes 1048576 | tf_op jit(solution)/shard_map/dense_backward/pallas_call | solution.py:351
  40.0 2.5 %add_bitcast_fusion = f32[2,2,48,1536]{3,2,1,0:T(8,128)} fusion(f32[2,2,2,48,1536]{4,3,2,1,0:T(8,128)} %bitcast.5, s32[]{:T(128)S(6)} %select_n.112, f32[2,2,2,48,1536]{4,3,2,1,0:T(8,128)S(1)} %bitcast.170), kind=kLoop, calls=%fused_computation.1 | loop fusion | flops 294912 | bytes 3538948 | tf_op jit(solution)/shard_map/add | solution.py:449
  42.5 2.5 %collective-permute-start.1 = (f32[2,2,48,1536]{3,2,1,0:T(8,128)}, f32[2,2,48,1536]{3,2,1,0:T(8,128)}, u32[]{:S(2)}, u32[]{:S(2)}) collective-permute-start(f32[2,2,48,1536]{3,2,1,0:T(8,128)} %add_bitcast_fusion), channel_id=1, source_target_pairs={{0,2},{1,5},{2,0},{3,7},{4,6},{5,1},{6,4},{7,3},{8,10},{9,13},{10,... | collective-permute-start | bytes 3538952 | tf_op jit(solution)/shard_map/sum_A_1/ppermute | solution.py:383
  45.2 14.6 %back_0.1 = (f32[8,1152]{1,0:T(8,128)}, bf16[4,3,384,256]{3,2,1,0:T(8,128)(2,1)}, f32[384,1152]{1,0:T(8,128)}, f32[384,1152]{1,0:T(8,128)}) custom-call(s32[4]{0:T(128)} %lengths_ref.9, s32[4]{0:T(128)} %pad_add_fusion.place_ref, bf16[4,768,256]{2,1,0:T(8,128)(2,1)} %get-tuple-element.128.first_ref, bf16[4,32,32,256]{3,2,1,0:T(8,128)(2,1)} %get-tuple-element.129.query_ref, ...), custom_call_target="tpu_custom_call" | custom-call | flops 125954949120 | bytes 1048576 | tf_op jit(solution)/shard_map/back_0/pallas_call | solution.py:351
  63.3 2.2 %bitcast_add_fusion = f32[2,48,1536]{2,1,0:T(8,128)} fusion(f32[2,2,48,1536]{3,2,1,0:T(8,128)} %collective-permute-done.1, s32[]{:T(128)S(6)} %select_n.115, f32[2,2,2,48,1536]{4,3,2,1,0:T(8,128)} %bitcast.5, s32[]{:T(128)S(6)} %select_n.114, s32[]{:T(128)S(6)} %select_n.116, f32[2,2,2,48,1536]{4,3,2,1,0:T(8,128)S(1)} %bitcast.171), kind=kLoop, calls=%fused_computation.10 | loop fusion | flops 294912 | bytes 2359308 | tf_op jit(solution)/shard_map/add | solution.py:449
  66.0 14.6 %back_1.1 = (f32[8,1152]{1,0:T(8,128)}, bf16[4,3,384,256]{3,2,1,0:T(8,128)(2,1)}, f32[384,1152]{1,0:T(8,128)}, f32[384,1152]{1,0:T(8,128)}) custom-call(s32[4]{0:T(128)} %lengths_ref.9, s32[4]{0:T(128)} %pad_add_fusion.place_ref, bf16[4,768,256]{2,1,0:T(8,128)(2,1)} %get-tuple-element.128.first_ref, bf16[4,32,32,256]{3,2,1,0:T(8,128)(2,1)} %get-tuple-element.129.query_ref, ...), custom_call_target="tpu_custom_call" | custom-call | flops 125954949120 | bytes 1048576 | tf_op jit(solution)/shard_map/back_1/pallas_call | solution.py:351
  93.5 2.8 %collective-permute-start.12 = (f32[48,768]{1,0:T(8,128)S(1)}, f32[48,768]{1,0:T(8,128)S(1)}, u32[]{:S(2)}, u32[]{:S(2)}) collective-permute-start(f32[48,768]{1,0:T(8,128)S(1)} %bitcast_add_fusion.18), channel_id=1, source_target_pairs={{0,8},{1,9},{2,10},{3,11},{4,12},{5,13},{6,14},{7,15},{8,0},{9,1},... | collective-permute-start | bytes 442376 | tf_op jit(solution)/shard_map/sum_O_3/ppermute | solution.py:383
  101.4 2.7 %collective-permute-start.10 = (f32[48,1536]{1,0:T(8,128)S(1)}, f32[48,1536]{1,0:T(8,128)S(1)}, u32[]{:S(2)}, u32[]{:S(2)}) collective-permute-start(f32[48,1536]{1,0:T(8,128)S(1)} %fusion), channel_id=1, source_target_pairs={{0,16},{1,17},{2,18},{3,19},{4,20},{5,21},{6,22},{7,23},{8,24},{9,... | collective-permute-start | bytes 884744 | tf_op jit(solution)/shard_map/sum_A_4/ppermute | solution.py:383
  105.9 7.5 %input.1 = (bf16[832,768]{1,0:T(8,128)(2,1)}, f32[16,768]{1,0:T(8,128)S(1)}) custom-call(s32[4]{0:T(128)S(1)} %copy-done.8, s32[4]{0:T(128)S(1)} %copy-done, bf16[832,768]{1,0:T(8,128)(2,1)S(1)} %copy-done.1, s32[832]{0:T(1024)S(1)} %copy-done.5, bf16[2,768]{1,0:T(2,128)(2,1)S(1)} %copy-done.6, bf16[768]{0:T(1024)(128)(2,1)S(1)} %copy-done.7, ...), custom_call_target="tpu_custom_call" | custom-call | flops 58888028160 | bytes 1048576 | tf_op jit(solution)/shard_map/input/pallas_call | solution.py:351
  119.7 3.6 %collective-permute-done.16 = f32[64,768]{1,0:T(8,128)S(1)} collective-permute-done((f32[64,768]{1,0:T(8,128)S(1)}, f32[64,768]{1,0:T(8,128)S(1)}, u32[]{:S(2)}, u32[]{:S(2)}) %collective-permute-start.16) | collective-permute-done | bytes 196640 | tf_op jit(solution)/shard_map/sum_O_4/ppermute | solution.py:383
  130.8 6.6 %collective-permute-done.20 = f32[48,1152]{1,0:T(8,128)S(1)} collective-permute-done((f32[48,1152]{1,0:T(8,128)S(1)}, f32[48,1152]{1,0:T(8,128)S(1)}, u32[]{:S(2)}, u32[]{:S(2)}) %collective-permute-start.20) | collective-permute-done | bytes 221216 | tf_op jit(solution)/shard_map/sum_B_3/ppermute | solution.py:383
  143.3 2.2 %collective-permute-start.21 = (f32[48,1152]{1,0:T(8,128)S(1)}, f32[48,1152]{1,0:T(8,128)S(1)}, u32[]{:S(2)}, u32[]{:S(2)}) collective-permute-start(f32[48,1152]{1,0:T(8,128)S(1)} %fusion.2), channel_id=1, source_target_pairs={{0,16},{1,17},{2,18},{3,19},{4,20},{5,21},{6,22},{7,23},{8,24},{9,... | collective-permute-start | bytes 663560 | tf_op jit(solution)/shard_map/sum_C_4/ppermute | solution.py:383
  145.5 5.6 %collective-permute-done.23 = f32[112,768]{1,0:T(8,128)S(1)} collective-permute-done((f32[112,768]{1,0:T(8,128)S(1)}, f32[112,768]{1,0:T(8,128)S(1)}, u32[]{:S(2)}, u32[]{:S(2)}) %collective-permute-start.23) | collective-permute-done | bytes 344096 | tf_op jit(solution)/shard_map/sum_O_6/ppermute | solution.py:383
  151.3 2.9 %collective-permute-done.22 = f32[48,1152]{1,0:T(8,128)S(1)} collective-permute-done((f32[48,1152]{1,0:T(8,128)S(1)}, f32[48,1152]{1,0:T(8,128)S(1)}, u32[]{:S(2)}, u32[]{:S(2)}) %collective-permute-start.22) | collective-permute-done | bytes 221216 | tf_op jit(solution)/shard_map/sum_B_4/ppermute | solution.py:383
  154.4 3.5 %collective-permute-done.21 = f32[48,1152]{1,0:T(8,128)S(1)} collective-permute-done((f32[48,1152]{1,0:T(8,128)S(1)}, f32[48,1152]{1,0:T(8,128)S(1)}, u32[]{:S(2)}, u32[]{:S(2)}) %collective-permute-start.21) | collective-permute-done | bytes 221216 | tf_op jit(solution)/shard_map/sum_C_4/ppermute | solution.py:383
  158.0 2.3 %collective-permute-done.27 = f32[48,1152]{1,0:T(8,128)S(1)} collective-permute-done((f32[48,1152]{1,0:T(8,128)S(1)}, f32[48,1152]{1,0:T(8,128)S(1)}, u32[]{:S(2)}, u32[]{:S(2)}) %collective-permute-start.27) | collective-permute-done | bytes 221216 | tf_op jit(solution)/shard_map/sum_B_5/ppermute | solution.py:383
  160.9 5.4 %collective-permute-done.24 = f32[48,1152]{1,0:T(8,128)S(1)} collective-permute-done((f32[48,1152]{1,0:T(8,128)S(1)}, f32[48,1152]{1,0:T(8,128)S(1)}, u32[]{:S(2)}, u32[]{:S(2)}) %collective-permute-start.24) | collective-permute-done | bytes 221216 | tf_op jit(solution)/shard_map/sum_C_5/ppermute | solution.py:383
  172.5 2.4 %place.5 = f32[2,2,2,2,48,768]{5,4,3,2,1,0:T(8,128)} custom-call(s32[4]{0:T(128)S(1)} %copy-done, f32[192,768]{1,0:T(8,128)S(1)} %bitcast.167, f32[208,768]{1,0:T(8,128)S(1)} %collective-permute-done.33.refs_1_, f32[192,768]{1,0:T(8,128)S(1)} %bitcast.154, f32[192,768]{1,0:T(8,128)S(1)} %slice.63), custom_call_target="tpu_custom_call" | custom-call | flops 10000000000 | bytes 1048576 | tf_op jit(solution)/shard_map/place/pallas_call | solution.py:425
  174.9 3.1 %place.6 = (f32[2,2,2,2,48,768]{5,4,3,2,1,0:T(8,128)}, f32[2,2,2,2,48,768]{5,4,3,2,1,0:T(8,128)}) custom-call(s32[4]{0:T(128)S(1)} %copy-done, f32[192,1536]{1,0:T(8,128)S(1)} %bitcast.159, f32[192,1536]{1,0:T(8,128)S(1)} %bitcast.160, f32[192,1536]{1,0:T(8,128)S(1)} %bitcast.155, f32[192,1536]{1,0:T(8,128)S(1)} %bitcast.158), custom_call_target="tpu_custom_call" | custom-call | flops 10000000000 | bytes 1048576 | tf_op jit(solution)/shard_map/place/pallas_call | solution.py:425
  178.0 3.8 %collective-permute-done.28 = f32[2,48,1152]{2,1,0:T(8,128)S(1)} collective-permute-done((f32[2,48,1152]{2,1,0:T(8,128)S(1)}, f32[2,48,1152]{2,1,0:T(8,128)S(1)}, u32[]{:S(2)}, u32[]{:S(2)}) %collective-permute-start.28) | collective-permute-done | bytes 442400 | tf_op jit(solution)/shard_map/sum_C_6/ppermute | solution.py:383
  181.9 3.8 %collective-permute-done.36 = f32[2,2,48,1152]{3,2,1,0:T(8,128)S(1)} collective-permute-done((f32[2,2,48,1152]{3,2,1,0:T(8,128)S(1)}, f32[2,2,48,1152]{3,2,1,0:T(8,128)S(1)}, u32[]{:S(2)}, u32[]{:S(2)}) %collective-permute-start.36) | collective-permute-done | bytes 884768 | tf_op jit(solution)/shard_map/sum_B_7/ppermute | solution.py:383
  188.2 2.7 %place.7 = (f32[2,2,2,2,48,768]{5,4,3,2,1,0:T(8,128)}, f32[2,2,2,2,48,768]{5,4,3,2,1,0:T(8,128)}, f32[2,2,2,2,48,768]{5,4,3,2,1,0:T(8,128)}) custom-call(s32[4]{0:T(128)S(1)} %copy-done, f32[192,1152]{1,0:T(8,128)S(1)} %bitcast.162, f32[192,1152]{1,0:T(8,128)S(1)} %bitcast.166, f32[192,1152]{1,0:T(8,128)S(1)} %bitcast.156, f32[192,1152]{1,0:T(8,128)S(1)} %bitcast.161), custom_call_target="tpu_custom_call" | custom-call | flops 10000000000 | bytes 1048576 | tf_op jit(solution)/shard_map/place/pallas_call | solution.py:425
  190.9 8.2 %collective-permute-done.34 = f32[2,2,48,1152]{3,2,1,0:T(8,128)S(1)} collective-permute-done((f32[2,2,48,1152]{3,2,1,0:T(8,128)S(1)}, f32[2,2,48,1152]{3,2,1,0:T(8,128)S(1)}, u32[]{:S(2)}, u32[]{:S(2)}) %collective-permute-start.34) | collective-permute-done | bytes 884768 | tf_op jit(solution)/shard_map/sum_C_7/ppermute | solution.py:383
  (148 shorter events, 58.5 us)
Async XLA Ops:
  27.1 12.8 %collective-permute-start = (f32[384,1536]{1,0:T(8,128)}, f32[384,1536]{1,0:T(8,128)}, u32[]{:S(2)}, u32[]{:S(2)}) collective-permute-start(f32[384,1536]{1,0:T(8,128)} %get-tuple-element.123), channel_id=1, source_target_pairs={{0,1},{1,0},{2,3},{3,2},{4,5},{5,4},{6,7},{7,6},{8,9},{9,8},{10,11... | collective-permute-start | bytes 7077896 | tf_op jit(solution)/shard_map/sum_A_0/ppermute | solution.py:383
  42.5 20.8 %collective-permute-start.1 = (f32[2,2,48,1536]{3,2,1,0:T(8,128)}, f32[2,2,48,1536]{3,2,1,0:T(8,128)}, u32[]{:S(2)}, u32[]{:S(2)}) collective-permute-start(f32[2,2,48,1536]{3,2,1,0:T(8,128)} %add_bitcast_fusion), channel_id=1, source_target_pairs={{0,2},{1,5},{2,0},{3,7},{4,6},{5,1},{6,4},{7,3},{8,10},{9,13},{10,... | collective-permute-start | bytes 3538952 | tf_op jit(solution)/shard_map/sum_A_1/ppermute | solution.py:383
  45.0 14.8 %collective-permute-start.2 = (f32[384,768]{1,0:T(8,128)}, f32[384,768]{1,0:T(8,128)}, u32[]{:S(2)}, u32[]{:S(2)}) collective-permute-start(f32[384,768]{1,0:T(8,128)} %get-tuple-element.137), channel_id=1, source_target_pairs={{0,1},{1,0},{2,3},{3,2},{4,5},{5,4},{6,7},{7,6},{8,9},{9,8},{10,11... | collective-permute-start | bytes 3538952 | tf_op jit(solution)/shard_map/sum_O_0/ppermute | solution.py:383
  61.8 18.9 %collective-permute-start.4 = (f32[2,2,48,768]{3,2,1,0:T(8,128)}, f32[2,2,48,768]{3,2,1,0:T(8,128)}, u32[]{:S(2)}, u32[]{:S(2)}) collective-permute-start(f32[2,2,48,768]{3,2,1,0:T(8,128)} %add_bitcast_fusion.3), channel_id=1, source_target_pairs={{0,2},{1,5},{2,0},{3,7},{4,6},{5,1},{6,4},{7,3},{8,10},{9,13},{10,... | collective-permute-start | bytes 1769480 | tf_op jit(solution)/shard_map/sum_O_1/ppermute | solution.py:383
  65.5 17.1 %collective-permute-start.3 = (f32[2,48,1536]{2,1,0:T(8,128)}, f32[2,48,1536]{2,1,0:T(8,128)}, u32[]{:S(2)}, u32[]{:S(2)}) collective-permute-start(f32[2,48,1536]{2,1,0:T(8,128)} %bitcast_add_fusion), channel_id=1, source_target_pairs={{0,4},{1,3},{2,6},{3,1},{4,0},{5,7},{6,2},{7,5},{8,12},{9,11},{10,... | collective-permute-start | bytes 1769480 | tf_op jit(solution)/shard_map/sum_A_2/ppermute | solution.py:383
  86.7 13.4 %collective-permute-start.5 = (f32[48,1536]{1,0:T(8,128)}, f32[48,1536]{1,0:T(8,128)S(1)}, u32[]{:S(2)}, u32[]{:S(2)}) collective-permute-start(f32[48,1536]{1,0:T(8,128)} %bitcast_add_fusion.3), channel_id=1, source_target_pairs={{0,8},{1,9},{2,10},{3,11},{4,12},{5,13},{6,14},{7,15},{8,0},{9,1},... | collective-permute-start | bytes 884744 | tf_op jit(solution)/shard_map/sum_A_3/ppermute | solution.py:383
  89.9 25.2 %collective-permute-start.11 = (f32[2,2,48,1152]{3,2,1,0:T(8,128)S(1)}, f32[2,2,48,1152]{3,2,1,0:T(8,128)S(1)}, u32[]{:S(2)}, u32[]{:S(2)}) collective-permute-start(f32[2,2,48,1152]{3,2,1,0:T(8,128)S(1)} %add_bitcast_fusion.2), channel_id=1, source_target_pairs={{0,2},{1,5},{2,0},{3,7},{4,6},{5,1},{6,4},{7,3},{8,10},{9,13},{10,... | collective-permute-start | bytes 2654216 | tf_op jit(solution)/shard_map/sum_B_1/ppermute | solution.py:383
  93.5 19.9 %collective-permute-start.12 = (f32[48,768]{1,0:T(8,128)S(1)}, f32[48,768]{1,0:T(8,128)S(1)}, u32[]{:S(2)}, u32[]{:S(2)}) collective-permute-start(f32[48,768]{1,0:T(8,128)S(1)} %bitcast_add_fusion.18), channel_id=1, source_target_pairs={{0,8},{1,9},{2,10},{3,11},{4,12},{5,13},{6,14},{7,15},{8,0},{9,1},... | collective-permute-start | bytes 442376 | tf_op jit(solution)/shard_map/sum_O_3/ppermute | solution.py:383
  98.1 19.5 %collective-permute-start.9 = (f32[2,2,48,1152]{3,2,1,0:T(8,128)S(1)}, f32[2,2,48,1152]{3,2,1,0:T(8,128)S(1)}, u32[]{:S(2)}, u32[]{:S(2)}) collective-permute-start(f32[2,2,48,1152]{3,2,1,0:T(8,128)S(1)} %add_bitcast_fusion.1), channel_id=1, source_target_pairs={{0,2},{1,5},{2,0},{3,7},{4,6},{5,1},{6,4},{7,3},{8,10},{9,13},{10,... | collective-permute-start | bytes 2654216 | tf_op jit(solution)/shard_map/sum_C_1/ppermute | solution.py:383
  101.4 15.3 %collective-permute-start.10 = (f32[48,1536]{1,0:T(8,128)S(1)}, f32[48,1536]{1,0:T(8,128)S(1)}, u32[]{:S(2)}, u32[]{:S(2)}) collective-permute-start(f32[48,1536]{1,0:T(8,128)S(1)} %fusion), channel_id=1, source_target_pairs={{0,16},{1,17},{2,18},{3,19},{4,20},{5,21},{6,22},{7,23},{8,24},{9,... | collective-permute-start | bytes 884744 | tf_op jit(solution)/shard_map/sum_A_4/ppermute | solution.py:383
  116.8 11.6 %collective-permute-start.14 = (f32[48,1536]{1,0:T(8,128)S(1)}, f32[48,1536]{1,0:T(8,128)S(1)}, u32[]{:S(2)}, u32[]{:S(2)}) collective-permute-start(f32[48,1536]{1,0:T(8,128)S(1)} %add.530), channel_id=1, source_target_pairs={{0,8},{1,9},{2,10},{3,11},{4,12},{5,13},{6,14},{7,15},{8,0},{9,1},... | collective-permute-start | bytes 884744 | tf_op jit(solution)/shard_map/sum_A_5/ppermute | solution.py:383
  123.4 16.6 %collective-permute-start.19 = (f32[64,768]{1,0:T(8,128)S(1)}, f32[64,768]{1,0:T(8,128)S(1)}, u32[]{:S(2)}, u32[]{:S(2)}) collective-permute-start(f32[64,768]{1,0:T(8,128)S(1)} %pad_maximum_fusion.12), channel_id=1, source_target_pairs={{0,8},{1,9},{2,10},{3,11},{4,12},{5,13},{6,14},{7,15},{8,0},{9,1},... | collective-permute-start | bytes 589832 | tf_op jit(solution)/shard_map/sum_O_5/ppermute | solution.py:383
  125.6 11.7 %collective-permute-start.20 = (f32[48,1152]{1,0:T(8,128)S(1)}, f32[48,1152]{1,0:T(8,128)S(1)}, u32[]{:S(2)}, u32[]{:S(2)}) collective-permute-start(f32[48,1152]{1,0:T(8,128)S(1)} %bitcast_add_fusion.13), channel_id=1, source_target_pairs={{0,8},{1,9},{2,10},{3,11},{4,12},{5,13},{6,14},{7,15},{8,0},{9,1},... | collective-permute-start | bytes 663560 | tf_op jit(solution)/shard_map/sum_B_3/ppermute | solution.py:383
  128.5 12.2 %collective-permute-start.18 = (f32[2,48,1536]{2,1,0:T(8,128)S(1)}, f32[2,48,1536]{2,1,0:T(8,128)S(1)}, u32[]{:S(2)}, u32[]{:S(2)}) collective-permute-start(f32[2,48,1536]{2,1,0:T(8,128)S(1)} %get-tuple-element.232), channel_id=1, source_target_pairs={{0,4},{1,3},{2,6},{3,1},{4,0},{5,7},{6,2},{7,5},{8,12},{9,11},{10,... | collective-permute-start | bytes 1769480 | tf_op jit(solution)/shard_map/sum_A_6/ppermute | solution.py:383
  138.4 15.8 %collective-permute-start.22 = (f32[48,1152]{1,0:T(8,128)S(1)}, f32[48,1152]{1,0:T(8,128)S(1)}, u32[]{:S(2)}, u32[]{:S(2)}) collective-permute-start(f32[48,1152]{1,0:T(8,128)S(1)} %fusion.1), channel_id=1, source_target_pairs={{0,16},{1,17},{2,18},{3,19},{4,20},{5,21},{6,22},{7,23},{8,24},{9,... | collective-permute-start | bytes 663560 | tf_op jit(solution)/shard_map/sum_B_4/ppermute | solution.py:383
  140.8 19.6 %collective-permute-start.25 = (f32[2,2,48,1536]{3,2,1,0:T(8,128)S(1)}, f32[2,2,48,1536]{3,2,1,0:T(8,128)S(1)}, u32[]{:S(2)}, u32[]{:S(2)}) collective-permute-start(f32[2,2,48,1536]{3,2,1,0:T(8,128)S(1)} %pad_maximum_fusion), channel_id=1, source_target_pairs={{0,2},{1,5},{2,0},{3,7},{4,6},{5,1},{6,4},{7,3},{8,10},{9,13},{10,... | collective-permute-start | bytes 3538952 | tf_op jit(solution)/shard_map/sum_A_7/ppermute | solution.py:383
  142.3 18.6 %collective-permute-start.26 = (f32[2,2,48,1536]{3,2,1,0:T(8,128)S(1)}, f32[2,2,48,1536]{3,2,1,0:T(8,128)S(1)}, u32[]{:S(2)}, u32[]{:S(2)}) collective-permute-start(f32[2,2,48,1536]{3,2,1,0:T(8,128)S(1)} %pad_maximum_fusion), channel_id=1, source_target_pairs={{0,1},{1,0},{2,3},{3,2},{4,5},{5,4},{6,7},{7,6},{8,9},{9,8},{10,11... | collective-permute-start | bytes 3538952 | tf_op jit(solution)/shard_map/sum_A_7/ppermute | solution.py:383
  143.3 14.7 %collective-permute-start.21 = (f32[48,1152]{1,0:T(8,128)S(1)}, f32[48,1152]{1,0:T(8,128)S(1)}, u32[]{:S(2)}, u32[]{:S(2)}) collective-permute-start(f32[48,1152]{1,0:T(8,128)S(1)} %fusion.2), channel_id=1, source_target_pairs={{0,16},{1,17},{2,18},{3,19},{4,20},{5,21},{6,22},{7,23},{8,24},{9,... | collective-permute-start | bytes 663560 | tf_op jit(solution)/shard_map/sum_C_4/ppermute | solution.py:383
  154.3 13.8 %collective-permute-start.31 = (f32[208,768]{1,0:T(8,128)S(1)}, f32[208,768]{1,0:T(8,128)S(1)}, u32[]{:S(2)}, u32[]{:S(2)}) collective-permute-start(f32[208,768]{1,0:T(8,128)S(1)} %pad_maximum_fusion.3), channel_id=1, source_target_pairs={{0,2},{1,5},{2,0},{3,7},{4,6},{5,1},{6,4},{7,3},{8,10},{9,13},{10,... | collective-permute-start | bytes 1916936 | tf_op jit(solution)/shard_map/sum_O_7/ppermute | solution.py:383
  168.8 13.0 %collective-permute-start.28 = (f32[2,48,1152]{2,1,0:T(8,128)S(1)}, f32[2,48,1152]{2,1,0:T(8,128)S(1)}, u32[]{:S(2)}, u32[]{:S(2)}) collective-permute-start(f32[2,48,1152]{2,1,0:T(8,128)S(1)} %get-tuple-element.234), channel_id=1, source_target_pairs={{0,4},{1,3},{2,6},{3,1},{4,0},{5,7},{6,2},{7,5},{8,12},{9,11},{10,... | collective-permute-start | bytes 1327112 | tf_op jit(solution)/shard_map/sum_C_6/ppermute | solution.py:383
  169.6 16.1 %collective-permute-start.36 = (f32[2,2,48,1152]{3,2,1,0:T(8,128)S(1)}, f32[2,2,48,1152]{3,2,1,0:T(8,128)S(1)}, u32[]{:S(2)}, u32[]{:S(2)}) collective-permute-start(f32[2,2,48,1152]{3,2,1,0:T(8,128)S(1)} %pad_maximum_fusion.1), channel_id=1, source_target_pairs={{0,2},{1,5},{2,0},{3,7},{4,6},{5,1},{6,4},{7,3},{8,10},{9,13},{10,... | collective-permute-start | bytes 2654216 | tf_op jit(solution)/shard_map/sum_B_7/ppermute | solution.py:383
  171.2 14.5 %collective-permute-start.37 = (f32[2,2,48,1152]{3,2,1,0:T(8,128)S(1)}, f32[2,2,48,1152]{3,2,1,0:T(8,128)S(1)}, u32[]{:S(2)}, u32[]{:S(2)}) collective-permute-start(f32[2,2,48,1152]{3,2,1,0:T(8,128)S(1)} %pad_maximum_fusion.1), channel_id=1, source_target_pairs={{0,1},{1,0},{2,3},{3,2},{4,5},{5,4},{6,7},{7,6},{8,9},{9,8},{10,11... | collective-permute-start | bytes 2654216 | tf_op jit(solution)/shard_map/sum_B_7/ppermute | solution.py:383
  186.1 13.0 %collective-permute-start.34 = (f32[2,2,48,1152]{3,2,1,0:T(8,128)S(1)}, f32[2,2,48,1152]{3,2,1,0:T(8,128)S(1)}, u32[]{:S(2)}, u32[]{:S(2)}) collective-permute-start(f32[2,2,48,1152]{3,2,1,0:T(8,128)S(1)} %pad_maximum_fusion.2), channel_id=1, source_target_pairs={{0,2},{1,5},{2,0},{3,7},{4,6},{5,1},{6,4},{7,3},{8,10},{9,13},{10,... | collective-permute-start | bytes 2654216 | tf_op jit(solution)/shard_map/sum_C_7/ppermute | solution.py:383
  187.2 12.0 %collective-permute-start.35 = (f32[2,2,48,1152]{3,2,1,0:T(8,128)S(1)}, f32[2,2,48,1152]{3,2,1,0:T(8,128)S(1)}, u32[]{:S(2)}, u32[]{:S(2)}) collective-permute-start(f32[2,2,48,1152]{3,2,1,0:T(8,128)S(1)} %pad_maximum_fusion.2), channel_id=1, source_target_pairs={{0,1},{1,0},{2,3},{3,2},{4,5},{5,4},{6,7},{7,6},{8,9},{9,8},{10,11... | collective-permute-start | bytes 2654216 | tf_op jit(solution)/shard_map/sum_C_7/ppermute | solution.py:383
  (35 other events, 324.4 us)
where the time goes:
time: 204 us
  Pallas kernels  87 us (43%)
  waiting for transfers between devices  53.7 us (26%)
  starting transfers between devices  33.1 us (16%)
  other arithmetic  25.5 us (12%)
  local copies, waits for them, and re-layouts  3.07 us (2%)
    pallas_call x5, Pallas kernels, call(): pl.pallas_call(kernel, grid_spec=pltpu.PrefetchScalarGridSpec(num_scalar_...  74.9 us
    ppermute x40, waiting for transfers between devices, swap(): lax.ppermute(values, AXES, [(i, i ^ 1 << (odd if i & 1 else even)) for i...  53.7 us
    ppermute x40, starting transfers between devices, swap(): lax.ppermute(values, AXES, [(i, i ^ 1 << (odd if i & 1 else even)) for i...  33.1 us
    add x12, other arithmetic, spread_sum(): functools.reduce(jnp.add, [pick(t, 1 - mine) for t in terms])  19.4 us
    pallas_call x5, Pallas kernels, put_in_place(): pl.pallas_call(functools.partial(place_kernel, parts, len(before)), grid_...  12.1 us
    add x4, other arithmetic, spread_sum(): total = functools.reduce(jnp.add, terms)  4.66 us
  transfers between devices with their start and end apart: 40, of which 16 were waited for; matrix products, arithmetic and copies ran while one was open for 12% of the time, Pallas kernels for 29%

commit v1 on v0

--- a/solution.py
+++ b/solution.py
@@ -88,7 +88,7 @@
 
 
 def attend_kernel(
-    factor, lengths_ref, place_ref, tokens_ref, kinds_ref, table_ref, gain_ref, shift_ref, query_bias_ref,
+    factor, lengths_ref, tokens_ref, kinds_ref, table_ref, gain_ref, shift_ref, query_bias_ref,
     value_bias_ref, query_weight_ref, key_weight_ref, value_weight_ref, output_bias_ref, inner_bias_ref,
     second_gain_ref, second_shift_ref, *refs,
 ):
@@ -119,7 +119,7 @@
         for copy in copies:
             copy.wait()
         feed_forward(
-            factor, lengths_ref, place_ref, edge_ref, table_ref, mixed_all_ref, *later, output_bias_ref,
+            factor, lengths_ref, edge_ref, table_ref, mixed_all_ref, *later, output_bias_ref,
             inner_bias_ref, second_gain_ref, second_shift_ref, *outputs, second_ref,
         )
 
@@ -179,7 +179,7 @@
 
 
 def feed_forward(
-    factor, lengths_ref, place_ref, edge_ref, table_ref, mixed_ref, tokens_ref, cotangent_ref, output_weight_ref,
+    factor, lengths_ref, edge_ref, table_ref, mixed_ref, tokens_ref, cotangent_ref, output_weight_ref,
     inner_weight_ref, outer_weight_ref, output_bias_ref, inner_bias_ref, gain_ref, shift_ref,
     middle_ref, act_ref, grad_inner_ref, kept_ref, sent_ref, second_ref,
 ):
@@ -200,18 +200,19 @@
     grad_inner_ref[...] = grad_inner
 
     second_ref[...] = second
-    for target, begin in core_halves(place_ref[0], kept_ref, sent_ref):
+    for target, begin in core_halves(kept_ref, sent_ref):
         target[:, :D] = dot(act_ref[:, pl.ds(begin, D // 2)], grad_low * BF16(factor), TN)
         target[:, D:] = dot(second_ref[:, pl.ds(begin, D // 2)], grad_inner * BF16(factor), TN)
 
 
-def core_halves(core, kept_ref, sent_ref):
+def core_halves(kept_ref, sent_ref):
     rows = kept_ref.shape[0]
+    core = lax.rem(lax.axis_index("narrow"), 2)
     return [(ref, pl.multiple_of(which * rows, 128)) for ref, which in ((kept_ref, core), (sent_ref, 1 - core))]
 
 
 def backward_kernel(
-    factor, lengths_ref, place_ref, middle_ref, act_ref, grad_inner_ref, mixed_ref, cotangent_ref, outer_bias_ref,
+    factor, lengths_ref, middle_ref, act_ref, grad_inner_ref, mixed_ref, cotangent_ref, outer_bias_ref,
     gain_ref, output_weight_ref, inner_weight_ref, outer_weight_ref,
     layer_ref, grad_middle_ref, grad_mixed_ref, kept_ref, sent_ref, vectors_ref,
 ):
@@ -228,7 +229,7 @@
     grads = [jnp.concatenate([grad_middle[i * SLOT : (i + 1) * SLOT], pad]).astype(BF16) for i in range(mols)]
     for i, grad in enumerate(grads):
         grad_mixed_ref[i] = dot(output_weight_ref[...], grad, NT).astype(BF16)
-    for target, begin in core_halves(place_ref[0], kept_ref, sent_ref):
+    for target, begin in core_halves(kept_ref, sent_ref):
         products = [dot(mixed_ref[i, pl.ds(begin, D // 2), :], grad * BF16(factor)) for i, grad in enumerate(grads)]
         target[...] = functools.reduce(jnp.add, products)
     layer = middle + dot(act_ref[...], outer_weight_ref[...]) + row_of(outer_bias_ref)
@@ -246,7 +247,7 @@
 
 
 def back_kernel(
-    factor, lengths_ref, place_ref, first_ref, query_ref, keys_ref, values_ref, mixed_ref, grad_ref, stat_ref,
+    factor, lengths_ref, first_ref, query_ref, keys_ref, values_ref, mixed_ref, grad_ref, stat_ref,
     vectors_ref, turned_grads_ref, kept_ref, sent_ref,
     mixed32_ref, grad32_ref, scores_ref, probs_ref, grads_ref,
 ):
@@ -287,13 +288,13 @@
     grads = grads_ref[...].astype(BF16)
     turned_grads_ref[0] = grads
     grads = (grads * BF16(factor)).reshape(3 * HALF, WIDE)
-    for target, begin in core_halves(place_ref[0], kept_ref, sent_ref):
+    for target, begin in core_halves(kept_ref, sent_ref):
         target[...] += dot(first_ref[0, pl.ds(begin, D // 2), :], grads, NT)
     vectors_ref[...] += dot(jnp.ones((8, WIDE), BF16), grads, NT)
 
 
 def input_kernel(
-    factor, lengths_ref, place_ref, tokens_ref, kinds_ref, table_ref, gain_ref, low_ref, high_ref, query_weight_ref,
+    factor, lengths_ref, tokens_ref, kinds_ref, table_ref, gain_ref, low_ref, high_ref, query_weight_ref,
     key_weight_ref, value_weight_ref, grad_middle_ref, dense_ref, low_bias_ref, high_bias_ref,
     tokens_grad_ref, vectors_ref,
     edge_ref,
@@ -351,7 +352,7 @@
     return pl.pallas_call(
         kernel,
         grid_spec=pltpu.PrefetchScalarGridSpec(
-            num_scalar_prefetch=2,
+            num_scalar_prefetch=1,
             grid=(count,),
             in_specs=in_specs,
             out_specs=out_specs,
@@ -540,7 +541,7 @@
     weight = whole(D, D)
     edges = pl.BlockSpec((rows,), lambda i, *_: (0,))
     column = pltpu.VMEM((rows, 1), F32)
-    scalars = (lengths, place)
+    scalars = (lengths,)
     once = pl.Buffered(1)
     single = lambda *shape: pl.BlockSpec(shape, lambda i, *_: (0,) * len(shape), pipeline_mode=once)
     now = lambda *shape: pl.BlockSpec((1,) + shape, lambda i, *_: (jnp.minimum(i, count - 1),) + (0,) * len(shape))

time: 204 us -> 203 us (level)
  no operation moved by 1% of the time
where the time goes in v1:
time: 203 us
  Pallas kernels  86.8 us (43%)
  waiting for transfers between devices  54.2 us (27%)
  starting transfers between devices  32.9 us (16%)
  other arithmetic  24.6 us (12%)
  local copies, waits for them, and re-layouts  3.07 us (2%)
    pallas_call x5, Pallas kernels, call(): pl.pallas_call(kernel, grid_spec=pltpu.PrefetchScalarGridSpec(num_scalar_...  74.7 us
    ppermute x40, waiting for transfers between devices, swap(): lax.ppermute(values, AXES, [(i, i ^ 1 << (odd if i & 1 else even)) for i...  54.2 us
    ppermute x40, starting transfers between devices, swap(): lax.ppermute(values, AXES, [(i, i ^ 1 << (odd if i & 1 else even)) for i...  32.9 us
    add x12, other arithmetic, spread_sum(): functools.reduce(jnp.add, [pick(t, 1 - mine) for t in terms])  19.1 us
    pallas_call x5, Pallas kernels, put_in_place(): pl.pallas_call(functools.partial(place_kernel, parts, len(before)), grid_...  12.1 us
    add x4, other arithmetic, spread_sum(): total = functools.reduce(jnp.add, terms)  4.57 us
  transfers between devices with their start and end apart: 40, of which 16 were waited for; matrix products, arithmetic and copies ran while one was open for 12% of the time, Pallas kernels for 29%

profile of v1, /device:TPU:0, one launch (start us, length us, event | category | flops | bytes accessed | tf_op | source)
XLA Modules:
  0.0 202.8 jit_solution(8041899419818805012)
XLA Ops:
  0.7 26.0 %attend.1 = (bf16[4,768,256]{2,1,0:T(8,128)(2,1)}, bf16[4,32,32,256]{3,2,1,0:T(8,128)(2,1)}, bf16[4,32,32,256]{3,2,1,0:T(8,128)(2,1)}, bf16[4,32,32,256]{3,2,1,0...) custom-call(s32[4]{0:T(128)} %lengths_ref.9, ...), custom_call_target="tpu_custom_call" | custom-call | flops 263360348160 | bytes 1048576 | tf_op jit(solution)/shard_map/attend/pallas_call | solution.py:352
  27.2 12.2 %dense_backward.1 = (bf16[832,768]{1,0:T(8,128)(2,1)}, f32[832,768]{1,0:T(8,128)}, bf16[4,768,256]{2,1,0:T(8,128)(2,1)}, f32[384,768]{1,0:T(8,128)}, f32[384,768]{1,0:T(8,128)}, /*index=5*/f32[8,768]{1,0:T(8,128)}) custom-call(s32[4]{0:T(128)} %lengths_ref.9, f32[832,768]{1,0:T(8,128)} %get-tuple-element.120.middle_ref, ...), custom_call_target="tpu_custom_call" | custom-call | flops 78517370880 | bytes 1048576 | tf_op jit(solution)/shard_map/dense_backward/pallas_call | solution.py:352
  39.5 2.4 %add_bitcast_fusion = f32[2,2,48,1536]{3,2,1,0:T(8,128)} fusion(f32[2,2,2,48,1536]{4,3,2,1,0:T(8,128)} %bitcast.1, s32[]{:T(128)S(6)} %select_n.111, f32[2,2,2,48,1536]{4,3,2,1,0:T(8,128)S(1)} %bitcast.170), kind=kLoop, calls=%fused_computation.1 | loop fusion | flops 294912 | bytes 3538948 | tf_op jit(solution)/shard_map/add | solution.py:450
  41.9 2.5 %collective-permute-start.1 = (f32[2,2,48,1536]{3,2,1,0:T(8,128)}, f32[2,2,48,1536]{3,2,1,0:T(8,128)}, u32[]{:S(2)}, u32[]{:S(2)}) collective-permute-start(f32[2,2,48,1536]{3,2,1,0:T(8,128)} %add_bitcast_fusion), channel_id=1, source_target_pairs={{0,2},{1,5},{2,0},{3,7},{4,6},{5,1},{6,4},{7,3},{8,10},{9,13},{10,... | collective-permute-start | bytes 3538952 | tf_op jit(solution)/shard_map/sum_A_1/ppermute | solution.py:384
  44.6 14.5 %back_0.1 = (f32[8,1152]{1,0:T(8,128)}, bf16[4,3,384,256]{3,2,1,0:T(8,128)(2,1)}, f32[384,1152]{1,0:T(8,128)}, f32[384,1152]{1,0:T(8,128)}) custom-call(s32[4]{0:T(128)} %lengths_ref.9, bf16[4,768,256]{2,1,0:T(8,128)(2,1)} %get-tuple-element.128.first_ref, bf16[4,32,32,256]{3,2,1,0:T(8,128)(2,1)} %get-tuple-element.129.query_ref, ...), custom_call_target="tpu_custom_call" | custom-call | flops 125954949120 | bytes 1048576 | tf_op jit(solution)/shard_map/back_0/pallas_call | solution.py:352
  62.6 2.2 %bitcast_add_fusion = f32[2,48,1536]{2,1,0:T(8,128)} fusion(f32[2,2,48,1536]{3,2,1,0:T(8,128)} %collective-permute-done.1, s32[]{:T(128)S(6)} %select_n.115, f32[2,2,2,48,1536]{4,3,2,1,0:T(8,128)} %bitcast.1, s32[]{:T(128)S(6)} %select_n.113, s32[]{:T(128)S(6)} %select_n.116, f32[2,2,2,48,1536]{4,3,2,1,0:T(8,128)S(1)} %bitcast.171), kind=kLoop, calls=%fused_computation.10 | loop fusion | flops 294912 | bytes 2359308 | tf_op jit(solution)/shard_map/add | solution.py:450
  65.2 14.5 %back_1.1 = (f32[8,1152]{1,0:T(8,128)}, bf16[4,3,384,256]{3,2,1,0:T(8,128)(2,1)}, f32[384,1152]{1,0:T(8,128)}, f32[384,1152]{1,0:T(8,128)}) custom-call(s32[4]{0:T(128)} %lengths_ref.9, bf16[4,768,256]{2,1,0:T(8,128)(2,1)} %get-tuple-element.128.first_ref, bf16[4,32,32,256]{3,2,1,0:T(8,128)(2,1)} %get-tuple-element.129.query_ref, ...), custom_call_target="tpu_custom_call" | custom-call | flops 125954949120 | bytes 1048576 | tf_op jit(solution)/shard_map/back_1/pallas_call | solution.py:352
  92.5 2.8 %collective-permute-start.12 = (f32[48,768]{1,0:T(8,128)S(1)}, f32[48,768]{1,0:T(8,128)S(1)}, u32[]{:S(2)}, u32[]{:S(2)}) collective-permute-start(f32[48,768]{1,0:T(8,128)S(1)} %bitcast_add_fusion.18), channel_id=1, source_target_pairs={{0,8},{1,9},{2,10},{3,11},{4,12},{5,13},{6,14},{7,15},{8,0},{9,1},... | collective-permute-start | bytes 442376 | tf_op jit(solution)/shard_map/sum_O_3/ppermute | solution.py:384
  100.5 2.7 %collective-permute-start.10 = (f32[48,1536]{1,0:T(8,128)S(1)}, f32[48,1536]{1,0:T(8,128)S(1)}, u32[]{:S(2)}, u32[]{:S(2)}) collective-permute-start(f32[48,1536]{1,0:T(8,128)S(1)} %fusion), channel_id=1, source_target_pairs={{0,16},{1,17},{2,18},{3,19},{4,20},{5,21},{6,22},{7,23},{8,24},{9,... | collective-permute-start | bytes 884744 | tf_op jit(solution)/shard_map/sum_A_4/ppermute | solution.py:384
  105.0 7.5 %input.1 = (bf16[832,768]{1,0:T(8,128)(2,1)}, f32[16,768]{1,0:T(8,128)S(1)}) custom-call(s32[4]{0:T(128)S(1)} %copy-done.7, bf16[832,768]{1,0:T(8,128)(2,1)S(1)} %copy-done, s32[832]{0:T(1024)S(1)} %copy-done.4, bf16[2,768]{1,0:T(2,128)(2,1)S(1)} %copy-done.5, bf16[768]{0:T(1024)(128)(2,1)S(1)} %copy-done.6, bf16[4,3,384,256]{3,2,1,0:T(8,128)(2,1)S(1)} %copy-done.9, ...), custom_call_target="tpu_custom_call" | custom-call | flops 58888028160 | bytes 1048576 | tf_op jit(solution)/shard_map/input/pallas_call | solution.py:352
  118.6 3.7 %collective-permute-done.16 = f32[64,768]{1,0:T(8,128)S(1)} collective-permute-done((f32[64,768]{1,0:T(8,128)S(1)}, f32[64,768]{1,0:T(8,128)S(1)}, u32[]{:S(2)}, u32[]{:S(2)}) %collective-permute-start.16) | collective-permute-done | bytes 196640 | tf_op jit(solution)/shard_map/sum_O_4/ppermute | solution.py:384
  129.7 6.6 %collective-permute-done.20 = f32[48,1152]{1,0:T(8,128)S(1)} collective-permute-done((f32[48,1152]{1,0:T(8,128)S(1)}, f32[48,1152]{1,0:T(8,128)S(1)}, u32[]{:S(2)}, u32[]{:S(2)}) %collective-permute-start.20) | collective-permute-done | bytes 221216 | tf_op jit(solution)/shard_map/sum_B_3/ppermute | solution.py:384
  142.3 2.2 %collective-permute-start.21 = (f32[48,1152]{1,0:T(8,128)S(1)}, f32[48,1152]{1,0:T(8,128)S(1)}, u32[]{:S(2)}, u32[]{:S(2)}) collective-permute-start(f32[48,1152]{1,0:T(8,128)S(1)} %fusion.2), channel_id=1, source_target_pairs={{0,16},{1,17},{2,18},{3,19},{4,20},{5,21},{6,22},{7,23},{8,24},{9,... | collective-permute-start | bytes 663560 | tf_op jit(solution)/shard_map/sum_C_4/ppermute | solution.py:384
  144.5 5.7 %collective-permute-done.23 = f32[112,768]{1,0:T(8,128)S(1)} collective-permute-done((f32[112,768]{1,0:T(8,128)S(1)}, f32[112,768]{1,0:T(8,128)S(1)}, u32[]{:S(2)}, u32[]{:S(2)}) %collective-permute-start.23) | collective-permute-done | bytes 344096 | tf_op jit(solution)/shard_map/sum_O_6/ppermute | solution.py:384
  150.3 3.0 %collective-permute-done.22 = f32[48,1152]{1,0:T(8,128)S(1)} collective-permute-done((f32[48,1152]{1,0:T(8,128)S(1)}, f32[48,1152]{1,0:T(8,128)S(1)}, u32[]{:S(2)}, u32[]{:S(2)}) %collective-permute-start.22) | collective-permute-done | bytes 221216 | tf_op jit(solution)/shard_map/sum_B_4/ppermute | solution.py:384
  153.5 3.5 %collective-permute-done.21 = f32[48,1152]{1,0:T(8,128)S(1)} collective-permute-done((f32[48,1152]{1,0:T(8,128)S(1)}, f32[48,1152]{1,0:T(8,128)S(1)}, u32[]{:S(2)}, u32[]{:S(2)}) %collective-permute-start.21) | collective-permute-done | bytes 221216 | tf_op jit(solution)/shard_map/sum_C_4/ppermute | solution.py:384
  157.1 2.3 %collective-permute-done.27 = f32[48,1152]{1,0:T(8,128)S(1)} collective-permute-done((f32[48,1152]{1,0:T(8,128)S(1)}, f32[48,1152]{1,0:T(8,128)S(1)}, u32[]{:S(2)}, u32[]{:S(2)}) %collective-permute-start.27) | collective-permute-done | bytes 221216 | tf_op jit(solution)/shard_map/sum_B_5/ppermute | solution.py:384
  159.9 5.5 %collective-permute-done.24 = f32[48,1152]{1,0:T(8,128)S(1)} collective-permute-done((f32[48,1152]{1,0:T(8,128)S(1)}, f32[48,1152]{1,0:T(8,128)S(1)}, u32[]{:S(2)}, u32[]{:S(2)}) %collective-permute-start.24) | collective-permute-done | bytes 221216 | tf_op jit(solution)/shard_map/sum_C_5/ppermute | solution.py:384
  171.7 2.4 %place.5 = f32[2,2,2,2,48,768]{5,4,3,2,1,0:T(8,128)} custom-call(s32[4]{0:T(128)S(1)} %pad_add_fusion.place_ref, f32[192,768]{1,0:T(8,128)S(1)} %bitcast.167, f32[208,768]{1,0:T(8,128)S(1)} %collective-permute-done.33.refs_1_, f32[192,768]{1,0:T(8,128)S(1)} %bitcast.154, f32[192,768]{1,0:T(8,128)S(1)} %slice.63), custom_call_target="tpu_custom_call" | custom-call | flops 10000000000 | bytes 1048576 | tf_op jit(solution)/shard_map/place/pallas_call | solution.py:426
  174.0 3.1 %place.6 = (f32[2,2,2,2,48,768]{5,4,3,2,1,0:T(8,128)}, f32[2,2,2,2,48,768]{5,4,3,2,1,0:T(8,128)}) custom-call(s32[4]{0:T(128)S(1)} %pad_add_fusion.place_ref, f32[192,1536]{1,0:T(8,128)S(1)} %bitcast.159, f32[192,1536]{1,0:T(8,128)S(1)} %bitcast.160, f32[192,1536]{1,0:T(8,128)S(1)} %bitcast.155, f32[192,1536]{1,0:T(8,128)S(1)} %bitcast.158), custom_call_target="tpu_custom_call" | custom-call | flops 10000000000 | bytes 1048576 | tf_op jit(solution)/shard_map/place/pallas_call | solution.py:426
  177.2 3.9 %collective-permute-done.28 = f32[2,48,1152]{2,1,0:T(8,128)S(1)} collective-permute-done((f32[2,48,1152]{2,1,0:T(8,128)S(1)}, f32[2,48,1152]{2,1,0:T(8,128)S(1)}, u32[]{:S(2)}, u32[]{:S(2)}) %collective-permute-start.28) | collective-permute-done | bytes 442400 | tf_op jit(solution)/shard_map/sum_C_6/ppermute | solution.py:384
  181.1 3.9 %collective-permute-done.36 = f32[2,2,48,1152]{3,2,1,0:T(8,128)S(1)} collective-permute-done((f32[2,2,48,1152]{3,2,1,0:T(8,128)S(1)}, f32[2,2,48,1152]{3,2,1,0:T(8,128)S(1)}, u32[]{:S(2)}, u32[]{:S(2)}) %collective-permute-start.36) | collective-permute-done | bytes 884768 | tf_op jit(solution)/shard_map/sum_B_7/ppermute | solution.py:384
  187.4 2.7 %place.7 = (f32[2,2,2,2,48,768]{5,4,3,2,1,0:T(8,128)}, f32[2,2,2,2,48,768]{5,4,3,2,1,0:T(8,128)}, f32[2,2,2,2,48,768]{5,4,3,2,1,0:T(8,128)}) custom-call(s32[4]{0:T(128)S(1)} %pad_add_fusion.place_ref, f32[192,1152]{1,0:T(8,128)S(1)} %bitcast.162, f32[192,1152]{1,0:T(8,128)S(1)} %bitcast.166, f32[192,1152]{1,0:T(8,128)S(1)} %bitcast.156, ...), custom_call_target="tpu_custom_call" | custom-call | flops 10000000000 | bytes 1048576 | tf_op jit(solution)/shard_map/place/pallas_call | solution.py:426
  190.2 8.1 %collective-permute-done.34 = f32[2,2,48,1152]{3,2,1,0:T(8,128)S(1)} collective-permute-done((f32[2,2,48,1152]{3,2,1,0:T(8,128)S(1)}, f32[2,2,48,1152]{3,2,1,0:T(8,128)S(1)}, u32[]{:S(2)}, u32[]{:S(2)}) %collective-permute-start.34) | collective-permute-done | bytes 884768 | tf_op jit(solution)/shard_map/sum_C_7/ppermute | solution.py:384
  (146 shorter events, 57.7 us)
Async XLA Ops:
  26.7 12.7 %collective-permute-start = (f32[384,1536]{1,0:T(8,128)}, f32[384,1536]{1,0:T(8,128)}, u32[]{:S(2)}, u32[]{:S(2)}) collective-permute-start(f32[384,1536]{1,0:T(8,128)} %get-tuple-element.123), channel_id=1, source_target_pairs={{0,1},{1,0},{2,3},{3,2},{4,5},{5,4},{6,7},{7,6},{8,9},{9,8},{10,11... | collective-permute-start | bytes 7077896 | tf_op jit(solution)/shard_map/sum_A_0/ppermute | solution.py:384
  41.9 20.7 %collective-permute-start.1 = (f32[2,2,48,1536]{3,2,1,0:T(8,128)}, f32[2,2,48,1536]{3,2,1,0:T(8,128)}, u32[]{:S(2)}, u32[]{:S(2)}) collective-permute-start(f32[2,2,48,1536]{3,2,1,0:T(8,128)} %add_bitcast_fusion), channel_id=1, source_target_pairs={{0,2},{1,5},{2,0},{3,7},{4,6},{5,1},{6,4},{7,3},{8,10},{9,13},{10,... | collective-permute-start | bytes 3538952 | tf_op jit(solution)/shard_map/sum_A_1/ppermute | solution.py:384
  44.4 14.7 %collective-permute-start.2 = (f32[384,768]{1,0:T(8,128)}, f32[384,768]{1,0:T(8,128)}, u32[]{:S(2)}, u32[]{:S(2)}) collective-permute-start(f32[384,768]{1,0:T(8,128)} %get-tuple-element.137), channel_id=1, source_target_pairs={{0,1},{1,0},{2,3},{3,2},{4,5},{5,4},{6,7},{7,6},{8,9},{9,8},{10,11... | collective-permute-start | bytes 3538952 | tf_op jit(solution)/shard_map/sum_O_0/ppermute | solution.py:384
  61.1 18.7 %collective-permute-start.4 = (f32[2,2,48,768]{3,2,1,0:T(8,128)}, f32[2,2,48,768]{3,2,1,0:T(8,128)}, u32[]{:S(2)}, u32[]{:S(2)}) collective-permute-start(f32[2,2,48,768]{3,2,1,0:T(8,128)} %add_bitcast_fusion.3), channel_id=1, source_target_pairs={{0,2},{1,5},{2,0},{3,7},{4,6},{5,1},{6,4},{7,3},{8,10},{9,13},{10,... | collective-permute-start | bytes 1769480 | tf_op jit(solution)/shard_map/sum_O_1/ppermute | solution.py:384
  64.7 16.9 %collective-permute-start.3 = (f32[2,48,1536]{2,1,0:T(8,128)}, f32[2,48,1536]{2,1,0:T(8,128)}, u32[]{:S(2)}, u32[]{:S(2)}) collective-permute-start(f32[2,48,1536]{2,1,0:T(8,128)} %bitcast_add_fusion), channel_id=1, source_target_pairs={{0,4},{1,3},{2,6},{3,1},{4,0},{5,7},{6,2},{7,5},{8,12},{9,11},{10,... | collective-permute-start | bytes 1769480 | tf_op jit(solution)/shard_map/sum_A_2/ppermute | solution.py:384
  85.8 13.5 %collective-permute-start.5 = (f32[48,1536]{1,0:T(8,128)}, f32[48,1536]{1,0:T(8,128)S(1)}, u32[]{:S(2)}, u32[]{:S(2)}) collective-permute-start(f32[48,1536]{1,0:T(8,128)} %bitcast_add_fusion.3), channel_id=1, source_target_pairs={{0,8},{1,9},{2,10},{3,11},{4,12},{5,13},{6,14},{7,15},{8,0},{9,1},... | collective-permute-start | bytes 884744 | tf_op jit(solution)/shard_map/sum_A_3/ppermute | solution.py:384
  89.0 25.1 %collective-permute-start.11 = (f32[2,2,48,1152]{3,2,1,0:T(8,128)S(1)}, f32[2,2,48,1152]{3,2,1,0:T(8,128)S(1)}, u32[]{:S(2)}, u32[]{:S(2)}) collective-permute-start(f32[2,2,48,1152]{3,2,1,0:T(8,128)S(1)} %add_bitcast_fusion.2), channel_id=1, source_target_pairs={{0,2},{1,5},{2,0},{3,7},{4,6},{5,1},{6,4},{7,3},{8,10},{9,13},{10,... | collective-permute-start | bytes 2654216 | tf_op jit(solution)/shard_map/sum_B_1/ppermute | solution.py:384
  92.5 19.9 %collective-permute-start.12 = (f32[48,768]{1,0:T(8,128)S(1)}, f32[48,768]{1,0:T(8,128)S(1)}, u32[]{:S(2)}, u32[]{:S(2)}) collective-permute-start(f32[48,768]{1,0:T(8,128)S(1)} %bitcast_add_fusion.18), channel_id=1, source_target_pairs={{0,8},{1,9},{2,10},{3,11},{4,12},{5,13},{6,14},{7,15},{8,0},{9,1},... | collective-permute-start | bytes 442376 | tf_op jit(solution)/shard_map/sum_O_3/ppermute | solution.py:384
  97.1 19.5 %collective-permute-start.9 = (f32[2,2,48,1152]{3,2,1,0:T(8,128)S(1)}, f32[2,2,48,1152]{3,2,1,0:T(8,128)S(1)}, u32[]{:S(2)}, u32[]{:S(2)}) collective-permute-start(f32[2,2,48,1152]{3,2,1,0:T(8,128)S(1)} %add_bitcast_fusion.1), channel_id=1, source_target_pairs={{0,2},{1,5},{2,0},{3,7},{4,6},{5,1},{6,4},{7,3},{8,10},{9,13},{10,... | collective-permute-start | bytes 2654216 | tf_op jit(solution)/shard_map/sum_C_1/ppermute | solution.py:384
  100.5 15.1 %collective-permute-start.10 = (f32[48,1536]{1,0:T(8,128)S(1)}, f32[48,1536]{1,0:T(8,128)S(1)}, u32[]{:S(2)}, u32[]{:S(2)}) collective-permute-start(f32[48,1536]{1,0:T(8,128)S(1)} %fusion), channel_id=1, source_target_pairs={{0,16},{1,17},{2,18},{3,19},{4,20},{5,21},{6,22},{7,23},{8,24},{9,... | collective-permute-start | bytes 884744 | tf_op jit(solution)/shard_map/sum_A_4/ppermute | solution.py:384
  122.3 16.7 %collective-permute-start.19 = (f32[64,768]{1,0:T(8,128)S(1)}, f32[64,768]{1,0:T(8,128)S(1)}, u32[]{:S(2)}, u32[]{:S(2)}) collective-permute-start(f32[64,768]{1,0:T(8,128)S(1)} %pad_maximum_fusion.12), channel_id=1, source_target_pairs={{0,8},{1,9},{2,10},{3,11},{4,12},{5,13},{6,14},{7,15},{8,0},{9,1},... | collective-permute-start | bytes 589832 | tf_op jit(solution)/shard_map/sum_O_5/ppermute | solution.py:384
  124.6 11.7 %collective-permute-start.20 = (f32[48,1152]{1,0:T(8,128)S(1)}, f32[48,1152]{1,0:T(8,128)S(1)}, u32[]{:S(2)}, u32[]{:S(2)}) collective-permute-start(f32[48,1152]{1,0:T(8,128)S(1)} %bitcast_add_fusion.13), channel_id=1, source_target_pairs={{0,8},{1,9},{2,10},{3,11},{4,12},{5,13},{6,14},{7,15},{8,0},{9,1},... | collective-permute-start | bytes 663560 | tf_op jit(solution)/shard_map/sum_B_3/ppermute | solution.py:384
  127.4 12.4 %collective-permute-start.18 = (f32[2,48,1536]{2,1,0:T(8,128)S(1)}, f32[2,48,1536]{2,1,0:T(8,128)S(1)}, u32[]{:S(2)}, u32[]{:S(2)}) collective-permute-start(f32[2,48,1536]{2,1,0:T(8,128)S(1)} %get-tuple-element.232), channel_id=1, source_target_pairs={{0,4},{1,3},{2,6},{3,1},{4,0},{5,7},{6,2},{7,5},{8,12},{9,11},{10,... | collective-permute-start | bytes 1769480 | tf_op jit(solution)/shard_map/sum_A_6/ppermute | solution.py:384
  129.6 11.7 %collective-permute-start.17 = (f32[48,1152]{1,0:T(8,128)S(1)}, f32[48,1152]{1,0:T(8,128)S(1)}, u32[]{:S(2)}, u32[]{:S(2)}) collective-permute-start(f32[48,1152]{1,0:T(8,128)S(1)} %bitcast_add_fusion.10), channel_id=1, source_target_pairs={{0,8},{1,9},{2,10},{3,11},{4,12},{5,13},{6,14},{7,15},{8,0},{9,1},... | collective-permute-start | bytes 663560 | tf_op jit(solution)/shard_map/sum_C_3/ppermute | solution.py:384
  137.2 16.1 %collective-permute-start.22 = (f32[48,1152]{1,0:T(8,128)S(1)}, f32[48,1152]{1,0:T(8,128)S(1)}, u32[]{:S(2)}, u32[]{:S(2)}) collective-permute-start(f32[48,1152]{1,0:T(8,128)S(1)} %fusion.1), channel_id=1, source_target_pairs={{0,16},{1,17},{2,18},{3,19},{4,20},{5,21},{6,22},{7,23},{8,24},{9,... | collective-permute-start | bytes 663560 | tf_op jit(solution)/shard_map/sum_B_4/ppermute | solution.py:384
  139.9 19.6 %collective-permute-start.25 = (f32[2,2,48,1536]{3,2,1,0:T(8,128)S(1)}, f32[2,2,48,1536]{3,2,1,0:T(8,128)S(1)}, u32[]{:S(2)}, u32[]{:S(2)}) collective-permute-start(f32[2,2,48,1536]{3,2,1,0:T(8,128)S(1)} %pad_maximum_fusion), channel_id=1, source_target_pairs={{0,2},{1,5},{2,0},{3,7},{4,6},{5,1},{6,4},{7,3},{8,10},{9,13},{10,... | collective-permute-start | bytes 3538952 | tf_op jit(solution)/shard_map/sum_A_7/ppermute | solution.py:384
  141.3 18.6 %collective-permute-start.26 = (f32[2,2,48,1536]{3,2,1,0:T(8,128)S(1)}, f32[2,2,48,1536]{3,2,1,0:T(8,128)S(1)}, u32[]{:S(2)}, u32[]{:S(2)}) collective-permute-start(f32[2,2,48,1536]{3,2,1,0:T(8,128)S(1)} %pad_maximum_fusion), channel_id=1, source_target_pairs={{0,1},{1,0},{2,3},{3,2},{4,5},{5,4},{6,7},{7,6},{8,9},{9,8},{10,11... | collective-permute-start | bytes 3538952 | tf_op jit(solution)/shard_map/sum_A_7/ppermute | solution.py:384
  142.3 14.7 %collective-permute-start.21 = (f32[48,1152]{1,0:T(8,128)S(1)}, f32[48,1152]{1,0:T(8,128)S(1)}, u32[]{:S(2)}, u32[]{:S(2)}) collective-permute-start(f32[48,1152]{1,0:T(8,128)S(1)} %fusion.2), channel_id=1, source_target_pairs={{0,16},{1,17},{2,18},{3,19},{4,20},{5,21},{6,22},{7,23},{8,24},{9,... | collective-permute-start | bytes 663560 | tf_op jit(solution)/shard_map/sum_C_4/ppermute | solution.py:384
  153.4 13.9 %collective-permute-start.31 = (f32[208,768]{1,0:T(8,128)S(1)}, f32[208,768]{1,0:T(8,128)S(1)}, u32[]{:S(2)}, u32[]{:S(2)}) collective-permute-start(f32[208,768]{1,0:T(8,128)S(1)} %pad_maximum_fusion.3), channel_id=1, source_target_pairs={{0,2},{1,5},{2,0},{3,7},{4,6},{5,1},{6,4},{7,3},{8,10},{9,13},{10,... | collective-permute-start | bytes 1916936 | tf_op jit(solution)/shard_map/sum_O_7/ppermute | solution.py:384
  168.1 13.0 %collective-permute-start.28 = (f32[2,48,1152]{2,1,0:T(8,128)S(1)}, f32[2,48,1152]{2,1,0:T(8,128)S(1)}, u32[]{:S(2)}, u32[]{:S(2)}) collective-permute-start(f32[2,48,1152]{2,1,0:T(8,128)S(1)} %get-tuple-element.234), channel_id=1, source_target_pairs={{0,4},{1,3},{2,6},{3,1},{4,0},{5,7},{6,2},{7,5},{8,12},{9,11},{10,... | collective-permute-start | bytes 1327112 | tf_op jit(solution)/shard_map/sum_C_6/ppermute | solution.py:384
  168.8 16.2 %collective-permute-start.36 = (f32[2,2,48,1152]{3,2,1,0:T(8,128)S(1)}, f32[2,2,48,1152]{3,2,1,0:T(8,128)S(1)}, u32[]{:S(2)}, u32[]{:S(2)}) collective-permute-start(f32[2,2,48,1152]{3,2,1,0:T(8,128)S(1)} %pad_maximum_fusion.1), channel_id=1, source_target_pairs={{0,2},{1,5},{2,0},{3,7},{4,6},{5,1},{6,4},{7,3},{8,10},{9,13},{10,... | collective-permute-start | bytes 2654216 | tf_op jit(solution)/shard_map/sum_B_7/ppermute | solution.py:384
  170.4 14.6 %collective-permute-start.37 = (f32[2,2,48,1152]{3,2,1,0:T(8,128)S(1)}, f32[2,2,48,1152]{3,2,1,0:T(8,128)S(1)}, u32[]{:S(2)}, u32[]{:S(2)}) collective-permute-start(f32[2,2,48,1152]{3,2,1,0:T(8,128)S(1)} %pad_maximum_fusion.1), channel_id=1, source_target_pairs={{0,1},{1,0},{2,3},{3,2},{4,5},{5,4},{6,7},{7,6},{8,9},{9,8},{10,11... | collective-permute-start | bytes 2654216 | tf_op jit(solution)/shard_map/sum_B_7/ppermute | solution.py:384
  185.2 13.0 %collective-permute-start.34 = (f32[2,2,48,1152]{3,2,1,0:T(8,128)S(1)}, f32[2,2,48,1152]{3,2,1,0:T(8,128)S(1)}, u32[]{:S(2)}, u32[]{:S(2)}) collective-permute-start(f32[2,2,48,1152]{3,2,1,0:T(8,128)S(1)} %pad_maximum_fusion.2), channel_id=1, source_target_pairs={{0,2},{1,5},{2,0},{3,7},{4,6},{5,1},{6,4},{7,3},{8,10},{9,13},{10,... | collective-permute-start | bytes 2654216 | tf_op jit(solution)/shard_map/sum_C_7/ppermute | solution.py:384
  186.3 12.0 %collective-permute-start.35 = (f32[2,2,48,1152]{3,2,1,0:T(8,128)S(1)}, f32[2,2,48,1152]{3,2,1,0:T(8,128)S(1)}, u32[]{:S(2)}, u32[]{:S(2)}) collective-permute-start(f32[2,2,48,1152]{3,2,1,0:T(8,128)S(1)} %pad_maximum_fusion.2), channel_id=1, source_target_pairs={{0,1},{1,0},{2,3},{3,2},{4,5},{5,4},{6,7},{7,6},{8,9},{9,8},{10,11... | collective-permute-start | bytes 2654216 | tf_op jit(solution)/shard_map/sum_C_7/ppermute | solution.py:384
  (34 other events, 316.2 us)
